TPU v7x, 256 devices: a whole 4x4x8 slice. The times are simulated.
256 devices in a mesh: uly: 4 (over x_hi, core), blk: 64 (over x_lo, y, z).
Axes of the slice: x: 4 (x_hi: 2, x_lo: 2; x = x_hi * 2 + x_lo), y: 4, z: 8, core: 2. Of those that a mesh axis runs over, the one named last changes fastest.
Arguments:
- queries: bfloat16 [8192, 3072], P(('blk', 'uly')), may hold values from -160 to 160
- keys: bfloat16 [8192, 3072], P(('blk', 'uly')), may hold values from -8 to 8
- values: bfloat16 [8192, 3072], P(('blk', 'uly')), may hold values from -6 to 6
- block_mask: int32 [24, 64, 64], replicated, may hold values from 0 to 1, as said below
- plan: int32 [24], replicated, may hold values from 0 to 23, each once
Outputs:
- attended: bfloat16 [8192, 3072], P(('blk', 'uly'))
Inputs may be any that keep to these rules, and one draw needn't show every extreme that they name: `block_mask`: every head's diagonal blocks are 1. Each device along `blk` attends for exactly one block of 128 tokens (block b belongs to blk device b). Cut the heads into 4 groups of 6 consecutive heads; for two different runs and one group, at most 2 pairs of a head and a key block of the second run have a 1 in some query block of the first run, and in every group, for some first run every second run reaches 2.
All inputs are finite; a program needn't handle non-finite values.
Results may differ from a plain program's by a relative error of at most 0.0055.
Values may be sent and summed in bfloat16 or wider, within the bound.
A program may use at most 128 MiB of HBM per device.

v0:
```python
import math

import jax
import jax.numpy as jnp
from jax import lax
from jax.sharding import PartitionSpec as P

BT = 128


def body(queries, keys, values, block_mask, plan):
    heads = plan.shape[0]
    size = queries.shape[1] // heads
    count = queries.shape[0]
    q_tok = queries.reshape(count, heads, size)
    k_tok = keys.reshape(count, heads, size)
    v_tok = values.reshape(count, heads, size)
    q_head, k_head, v_head = (
        lax.all_to_all(q_tok, "uly", split_axis=1, concat_axis=0, tiled=True),
        lax.all_to_all(k_tok, "uly", split_axis=1, concat_axis=0, tiled=True),
        lax.all_to_all(v_tok, "uly", split_axis=1, concat_axis=0, tiled=True),
    )
    local = q_head.shape[1]
    rows = q_head.shape[0]
    per_dev = rows // BT
    here = lax.axis_index("blk")
    masks_loc = lax.dynamic_slice_in_dim(block_mask, lax.axis_index("uly") * local, local, 0)
    scale = 1.0 / math.sqrt(size)
    masks = lax.dynamic_slice_in_dim(masks_loc, here * per_dev, per_dev, 1)
    top = jnp.full((local, rows), -1e30, jnp.float32)
    k_piece = lax.all_gather(k_head, "blk", axis=0, tiled=True)
    v_piece = lax.all_gather(v_head, "blk", axis=0, tiled=True)
    allowed = jnp.repeat(jnp.repeat(masks, BT, axis=1), BT, axis=2) > 0
    score = jnp.einsum("qhd,khd->hqk", q_head, k_piece, preferred_element_type=jnp.float32) * scale
    score = jnp.where(allowed, score, -jnp.inf)
    new_top = jnp.maximum(top, jnp.max(score, axis=2))
    expo = jnp.exp(score - new_top[:, :, None])
    total = jnp.sum(expo, axis=2)
    update = jnp.einsum(
        "hqk,khd->hqd", expo.astype(jnp.bfloat16), v_piece, preferred_element_type=jnp.float32
    )
    mixed = update
    top, total, mixed = (new_top, total, mixed)
    result = (mixed / total[:, :, None]).astype(jnp.bfloat16)
    result = jnp.transpose(result, (1, 0, 2))
    back = lax.all_to_all(result, "uly", split_axis=0, concat_axis=1, tiled=True)
    back = jnp.take(back, plan, axis=1)
    return back.reshape(count, heads * size)


def solution(mesh):
    placed = (P(("blk", "uly"), None), P(("blk", "uly"), None), P(("blk", "uly"), None), P(), P())
    return jax.shard_map(
        body, mesh=mesh, in_specs=placed, out_specs=P(("blk", "uly"), None), check_vma=False
    )
```

profile of v0, /device:TPU:1, one launch (start us, length us, event | category | flops | bytes accessed | tf_op | source)
XLA Modules:
  0.0 703.7 jit_solution(14296115288001667691)
XLA Ops:
  6.5 0.0 copy-start
  6.5 0.0 all-gather.3.cloned.1.call-start
  6.5 1.0 copy_bitcast_fusion.2
  7.6 11.7 %all_to_all.72 = bf16[32,24,128]{2,0,1:T(8,128)(2,1)S(1)} all-to-all(bf16[32,24,128]{2,0,1:T(8,128)(2,1)S(1)} %copy_bitcast_fusion.2), channel_id=1, replica_groups=mesh['uly'=4,'blk'=64] {'uly'}, dimensions={1} | all-to-all | bytes 393216 | tf_op jit(solution)/shard_map/all_to_all | solution.py:20
  19.3 0.7 copy.33
  20.0 0.0 all-gather.3.cloned.1.call-update
  20.0 0.0 all-gather.5.cloned.1.call-start
  20.0 1.0 copy_bitcast_fusion.1
  21.0 9.2 %all_to_all.73 = bf16[32,24,128]{2,0,1:T(8,128)(2,1)S(1)} all-to-all(bf16[32,24,128]{2,0,1:T(8,128)(2,1)S(1)} %copy_bitcast_fusion.1), channel_id=1, replica_groups=mesh['uly'=4,'blk'=64] {'uly'}, dimensions={1} | all-to-all | bytes 393216 | tf_op jit(solution)/shard_map/all_to_all | solution.py:21
  30.2 0.7 copy.35
  30.9 0.0 all-gather.5.cloned.1.call-update
  30.9 1.6 copy_bitcast_fusion.3
  32.6 4.1 all-to-all-start
  36.6 0.0 copy-done
  36.7 0.1 broadcast_bitcast_fusion
  36.8 0.7 compare_and_fusion
  37.5 0.1 broadcast_bitcast_fusion.1
  37.6 5.1 all-to-all-done
  42.7 260.0 %all-gather.3.cloned.1.call-done = bf16[8192,6,128]{2,0,1:T(8,128)(2,1)} async-done(((bf16[128,6,128]{2,0,1:T(8,128)(2,1)}), bf16[8192,6,128]{2,0,1:T(8,128)(2,1)}) %all-gather.3.cloned.1.call-update) | async-done | bytes 12582928 | tf_op jit(solution)/shard_map/all_gather | solution.py:31
  302.8 12.9 %fusion = (f32[6,128]{1,0:T(8,128)S(1)}, f32[6,128,8192]{2,1,0:T(8,128)}) fusion(pred[6,8192]{1,0:T(8,128)(4,1)S(1)} %bitcast.56, bf16[128,6,128]{2,0,1:T(8,128)(2,1)S(1)} %bitcast.60, bf16[8192,6,128]{2,0,1:T(8,128)(2,1)} %all-gather.3.cloned.1.call-done), kind=kOutput, calls=%fused_computation.3 | convolution fusion | flops 1629486336 | bytes 37997568 | tf_op jit(solution)/shard_map/qhd,khd->hqk/dot_general | solution.py:34
  315.7 11.5 %fusion.1 = f32[6,128]{1,0:T(8,128)S(1)} fusion(f32[6,128,8192]{2,1,0:T(8,128)} %get-tuple-element.6, f32[6,128]{1,0:T(8,128)S(1)} %broadcast_maximum_fusion, pred[6,8192]{1,0:T(8,128)(4,1)S(1)} %bitcast.57), kind=kLoop, calls=%fused_computation.4 | loop fusion | flops 25165056 | bytes 25221120 | tf_op jit(solution)/shard_map/reduce_sum | solution.py:38
  327.2 297.0 %all-gather.5.cloned.1.call-done = bf16[8192,6,128]{2,0,1:T(8,128)(2,1)} async-done(((bf16[128,6,128]{2,0,1:T(8,128)(2,1)}), bf16[8192,6,128]{2,0,1:T(8,128)(2,1)}) %all-gather.5.cloned.1.call-update) | async-done | bytes 12582928 | tf_op jit(solution)/shard_map/all_gather | solution.py:32
  624.2 0.0 copy-start.1
  624.2 14.9 %fusion.15 = bf16[128,6,128]{2,0,1:T(8,128)(2,1)S(1)} fusion(bf16[8192,6,128]{2,0,1:T(8,128)(2,1)} %all-gather.5.cloned.1.call-done, f32[6,128,8192]{2,1,0:T(8,128)} %get-tuple-element.6, f32[6,128]{1,0:T(8,128)S(1)} %broadcast_maximum_fusion, pred[6,8192]{1,0:T(8,128)(4,1)S(1)} %bitcast.58, f32[128,6]{0,1:T(8,128)S(1)} %bitcast.67), kind=kOutput, calls=%fused_computation.13 | convolution fusion | flops 1635975168 | bytes 38000640 | tf_op jit(solution)/shard_map/hqk,khd->hqd/dot_general | solution.py:39
  639.1 0.8 copy.36
  640.0 48.9 %all-to-all-start.3 = ((bf16[128,6,128]{2,1,0:T(8,128)(2,1)}), bf16[128,6,128]{2,1,0:T(8,128)(2,1)S(1)}, u32[]{:S(2)}, u32[]{:S(2)}) async-start(bf16[128,6,128]{2,1,0:T(8,128)(2,1)} %copy.36), calls=%async_computation.3 | async-start | bytes 524288 | tf_op jit(solution)/shard_map/all_to_all | solution.py:46
  688.8 0.0 copy-done.1
  688.8 6.7 all-to-all-done.3
  695.5 0.6 gather_fusion
  696.1 0.7 bitcast_select_fusion
  (8 shorter events, 0.1 us)
Async XLA Ops:
  6.5 30.1 %copy-start = (s32[24,64,64]{2,1,0:T(8,128)S(1)}, s32[24,64,64]{2,1,0:T(8,128)}, u32[]{:S(2)}) copy-start(s32[24,64,64]{2,1,0:T(8,128)} %param.8) | copy-start | bytes 1179652
  6.5 296.2 %all-gather.3.cloned.1.call-start = ((), (), s32[]{:S(2)}) async-start(), calls=%async_computation.4 | async-start | bytes 12779520 | tf_op jit(solution)/shard_map/all_gather | solution.py:31
  20.0 604.2 %all-gather.5.cloned.1.call-start = ((), (), s32[]{:S(2)}) async-start(), calls=%async_computation.5 | async-start | bytes 12779520 | tf_op jit(solution)/shard_map/all_gather | solution.py:32
  32.6 10.2 %all-to-all-start = ((bf16[32,24,128]{2,0,1:T(8,128)(2,1)}), bf16[32,24,128]{2,0,1:T(8,128)(2,1)S(1)}, u32[]{:S(2)}, u32[]{:S(2)}) async-start(bf16[32,24,128]{2,0,1:T(8,128)(2,1)} %copy_bitcast_fusion.3), calls=%async_computation | async-start | bytes 393216 | tf_op jit(solution)/shard_map/all_to_all | solution.py:19
  624.2 64.6 %copy-start.1 = (s32[24]{0:T(128)S(1)}, s32[24]{0:T(128)}, u32[]{:S(2)}) copy-start(s32[24]{0:T(128)} %param.9) | copy-start | bytes 292
  640.0 55.5 %all-to-all-start.3 = ((bf16[128,6,128]{2,1,0:T(8,128)(2,1)}), bf16[128,6,128]{2,1,0:T(8,128)(2,1)S(1)}, u32[]{:S(2)}, u32[]{:S(2)}) async-start(bf16[128,6,128]{2,1,0:T(8,128)(2,1)} %copy.36), calls=%async_computation.3 | async-start | bytes 524288 | tf_op jit(solution)/shard_map/all_to_all | solution.py:46
Sparse Core Ops, SparseCore 0:
  20.1 282.6 all-gather.2
  304.6 319.5 all-gather.4
where the time goes:
time: 704 us
  waiting for transfers between devices  569 us (81%)
  starting transfers between devices  53 us (8%)
  matrix products  27.8 us (4%)
  blocking collectives  20.9 us (3%)
  between operations  13.5 us (2%)
  other arithmetic  12.9 us (2%)
    all_gather x1, waiting for transfers between devices, body(): v_piece = lax.all_gather(v_head, 'blk', axis=0, tiled=True)  297 us
    all_gather x1, waiting for transfers between devices, body(): k_piece = lax.all_gather(k_head, 'blk', axis=0, tiled=True)  260 us
    all_to_all x1, starting transfers between devices, body(): lax.all_to_all(result, 'uly', split_axis=0, concat_axis=1, tiled=True)  48.9 us
    dot_general x1, matrix products, body(): jnp.einsum('hqk,khd->hqd', expo.astype(jnp.bfloat16), v_piece, preferred_...  14.9 us
  transfers between devices with their start and end apart: 4, of which 4 were waited for; matrix products, arithmetic and copies ran while one was open for 4% of the time, Pallas kernels for 0%

commit v1 on v0

v1 whole, which is shorter than its diff:
```python
import functools
import math

import jax
import jax.numpy as jnp
from jax import lax
from jax.experimental import pallas as pl
from jax.experimental.pallas import tpu as pltpu
from jax.sharding import PartitionSpec as P

MESH = pl.DeviceIdType.MESH
HD = 128
BT = 128
NU = 4
NX, NY, NZ = 2, 4, 8
NR = NX * NY
HL = 6
HG = 2
NG = HL // HG
TD = BT // NU
HALF = NZ // 2
BIG = 1e30
NT = (((1,), (1,)), ((), ()))


def kernel(
    q_in, k_in, v_in, mask_s, plan_s, out_ref,
    k_st, v_st, q_st, k_buf, v_buf, q_buf, shade, acc, top, tot,
    ob, st, ob_in, st_in, fin, got,
    us, ur, ul, rs, rr, qs, qr, os_, or_, ss, sr, fs, fr,
):
    u = lax.axis_index("uly")
    b = lax.axis_index("blk")
    z = b % NZ
    y = (b // NZ) % NY
    x = b // (NZ * NY)
    scale = 1.0 / math.sqrt(HD)

    def blk_at(xx, yy, zz):
        return {"blk": ((xx % NX) * NY + yy % NY) * NZ + zz % NZ}

    def uly_at(k):
        return {"uly": (u + k) % NU}

    up, down = blk_at(x, y, z + 1), blk_at(x, y, z + NZ - 1)
    plane = [blk_at(x + r // NY, y + r % NY, z) for r in range(NR)]

    barrier = pltpu.get_barrier_semaphore()
    partners = [uly_at(k) for k in range(1, NU)] + [up, down] + plane[1:]
    for device in partners:
        pl.semaphore_signal(barrier, inc=1, device_id=device, device_id_type=MESH)
    pl.semaphore_wait(barrier, len(partners))

    def remote(src, dst, send, recv, device):
        return pltpu.make_async_remote_copy(
            src_ref=src, dst_ref=dst, send_sem=send, recv_sem=recv, device_id=device, device_id_type=MESH
        )

    ins = ((k_in, k_st), (v_in, v_st), (q_in, q_st))

    def own_in(g, a):
        src, dst = ins[a]
        columns = pl.ds(pl.multiple_of((u * HL + g * HG) * HD, HD), HG * HD)
        rows = pl.ds(pl.multiple_of(u * TD, TD), TD)
        return pltpu.make_async_copy(src.at[:, columns], dst.at[g, rows, :], ul.at[g, a])

    def uly_in(g, a, k):
        src, dst = ins[a]
        columns = pl.ds(pl.multiple_of((((u + k) % NU) * HL + g * HG) * HD, HD), HG * HD)
        rows = pl.ds(pl.multiple_of(u * TD, TD), TD)
        return remote(src.at[:, columns], dst.at[g, rows, :], us.at[g, a, k - 1], ur.at[g, a, k - 1], uly_at(k))

    def heads_of(g):
        return pl.ds(g * HG, HG)

    def ring(g, s, i):
        buf = k_buf if i < 2 else v_buf
        right = i % 2 == 0
        src = s - 1 if right else (NZ - s + 1) % NZ
        dst = s if right else NZ - s
        return remote(
            buf.at[src, heads_of(g)], buf.at[dst, heads_of(g)],
            rs.at[g, s - 1, i], rr.at[g, s - 1, i], up if right else down,
        )

    def lanes_of(s):
        return (0, 1, 2, 3) if s < HALF else (0, 3)

    def q_copy(g, j):
        if j == 0:
            src, dst, device = 0, NY, plane[NY]
        else:
            dy = (j - 1) % (NY - 1) + 1
            src = 0 if j < NY else NY
            dst, device = src + dy, blk_at(x, y + NY - dy, z)
        rows = lambda r: q_buf.at[heads_of(g), pl.ds(r * BT, BT), :]
        return remote(rows(src), rows(dst), qs.at[g, j], qr.at[g, j], device)

    def o_copy(g, r):
        return remote(ob.at[g, r], ob_in.at[g, r], os_.at[g, r - 1], or_.at[g, r - 1], plane[r])

    def st_copy(g, r):
        return remote(st.at[g, r], st_in.at[g, r], ss.at[g, r - 1], sr.at[g, r - 1], plane[r])

    def fin_copy(g, k):
        rows = pl.ds(pl.multiple_of(((u + k) % NU) * TD, TD), TD)
        return remote(
            fin.at[heads_of(g), rows, :], got.at[pl.ds(u * HL + g * HG, HG)],
            fs.at[g, k - 1], fr.at[g, k - 1], uly_at(k),
        )

    def arrive(g, a):
        own_in(g, a).wait()
        for k in range(1, NU):
            uly_in(g, a, k).wait_recv()

    def prepare(g):
        arrive(g, 0)
        for hh in range(HG):
            k_buf[0, g * HG + hh] = k_st[g, :, hh * HD:(hh + 1) * HD]
        arrive(g, 1)
        for hh in range(HG):
            v_buf[0, g * HG + hh] = v_st[g, :, hh * HD:(hh + 1) * HD].T
        arrive(g, 2)
        for hh in range(HG):
            q_buf[g * HG + hh, 0:BT, :] = q_st[g, :, hh * HD:(hh + 1) * HD]
        for j in range(NY):
            q_copy(g, j).start()

    def launch(g):
        for i in lanes_of(1):
            ring(g, 1, i).start()

    def relay(g):
        q_copy(g, 0).wait_recv()
        for j in range(NY, 2 * NY - 1):
            q_copy(g, j).start()

    def tick(g, s):
        for i in lanes_of(s):
            ring(g, s, i).wait_recv()
            if s < HALF and i in lanes_of(s + 1):
                ring(g, s + 1, i).start()

    def unit(g, slots, first=False):
        def head(hh, carry):
            h = g * HG + hh
            keys = jnp.concatenate([k_buf[t, h] for t in slots], axis=0)
            vals = jnp.concatenate([v_buf[t, h] for t in slots], axis=1)
            for pair in range(NR // 2):
                lanes = slice(pair * 2 * BT, (pair + 1) * 2 * BT)
                score = lax.dot_general(keys, q_buf[h, lanes, :], NT, preferred_element_type=jnp.float32)
                parts = [score[i * BT:(i + 1) * BT] for i in range(len(slots))]
                shades = [shade[h, t:t + 1, lanes] for t in slots]
                tops = [jnp.minimum(jnp.max(p, axis=0, keepdims=True), -m) for p, m in zip(parts, shades)]
                new_top = functools.reduce(jnp.maximum, tops)
                if not first:
                    old_top = top[h, :, lanes]
                    new_top = jnp.maximum(new_top, old_top)
                    fade = jnp.exp((old_top - new_top) * scale)
                expo = [jnp.exp((p - jnp.maximum(new_top, m)) * scale) for p, m in zip(parts, shades)]
                total = sum(jnp.sum(e, axis=0, keepdims=True) for e in expo)
                weight = jnp.concatenate([e.astype(jnp.bfloat16) for e in expo], axis=0)
                update = jnp.dot(vals, weight, preferred_element_type=jnp.float32)
                if not first:
                    update = update + acc[h, :, lanes] * fade
                    total = total + tot[h, :, lanes] * fade
                acc[h, :, lanes] = update
                tot[h, :, lanes] = total
                top[h, :, lanes] = new_top
            return carry

        lax.fori_loop(0, HG, head, 0)

    def give_back(g):
        for r in range(1, NR):
            lanes = slice(r * BT, (r + 1) * BT)
            for hh in range(HG):
                h = g * HG + hh
                ob[g, r, hh * HD:(hh + 1) * HD, :] = acc[h, :, lanes].astype(jnp.bfloat16)
                st[g, r, 2 * hh:2 * hh + 1, :] = top[h, :, lanes]
                st[g, r, 2 * hh + 1:2 * hh + 2, :] = tot[h, :, lanes]
            st_copy(g, r).start()
            o_copy(g, r).start()

    def combine(g):
        for r in range(1, NR):
            st_copy(g, r).wait_recv()
            o_copy(g, r).wait_recv()
        for hh in range(HG):
            h = g * HG + hh
            tops = [top[h, :, 0:BT]] + [st_in[g, r, 2 * hh:2 * hh + 1, :] for r in range(1, NR)]
            tots = [tot[h, :, 0:BT]] + [st_in[g, r, 2 * hh + 1:2 * hh + 2, :] for r in range(1, NR)]
            best = functools.reduce(jnp.maximum, tops)
            fades = [jnp.exp((t - best) * scale) for t in tops]
            total = sum(f * t for f, t in zip(fades, tots))
            mixed = acc[h, :, 0:BT] * fades[0]
            for r in range(1, NR):
                mixed = mixed + ob_in[g, r, hh * HD:(hh + 1) * HD, :].astype(jnp.float32) * fades[r]
            fin[h] = (mixed / total).T.astype(jnp.bfloat16)
            got[u * HL + h] = fin[h, pl.ds(pl.multiple_of(u * TD, TD), TD), :]
        for k in range(1, NU):
            fin_copy(g, k).start()

    for g in range(NG):
        for a in range(3):
            for k in range(1, NU):
                uly_in(g, a, k).start()
            own_in(g, a).start()

    def shades(h, carry):
        for t in range(NZ):
            for r in range(NR):
                where = ((x + r // NY) % NX) * NY + (y + r % NY) % NY
                allowed = mask_s[h * (NR * NZ) + where * NZ + (z + NZ - t) % NZ]
                value = jnp.where(allowed > 0, -BIG, BIG).astype(jnp.float32)
                shade[h, t:t + 1, r * BT:(r + 1) * BT] = jnp.full((1, BT), value, jnp.float32)
        return carry

    lax.fori_loop(0, HL, shades, 0)
    prepare(0)
    launch(0)

    def group(g, carry):
        tick(g, 1)

        @pl.when(g == 0)
        def _():
            relay(g)

        @pl.when(g + 1 < NG)
        def _():
            prepare(g + 1)

        tick(g, 2)
        for j in range(1, 2 * NY - 1):
            q_copy(g, j).wait_recv()
        unit(g, (0,), first=True)
        unit(g, (1, 7))
        tick(g, 3)

        @pl.when(g + 1 < NG)
        def _():
            launch(g + 1)
            relay(g + 1)

        unit(g, (2, 6))

        @pl.when(g > 0)
        def _():
            combine(g - 1)

        unit(g, (3, 5))
        tick(g, 4)
        unit(g, (4,))
        give_back(g)
        return carry

    lax.fori_loop(0, NG, group, 0)
    combine(NG - 1)
    for g in range(NG):
        for k in range(1, NU):
            fin_copy(g, k).wait_recv()
    for s in range(NU * HL):
        out_ref[:, s * HD:(s + 1) * HD] = got[plan_s[s]]

    def drain(g, carry):
        for a in range(3):
            for k in range(1, NU):
                uly_in(g, a, k).wait_send()
        for s in range(1, HALF + 1):
            for i in lanes_of(s):
                ring(g, s, i).wait_send()
        for j in range(2 * NY - 1):
            q_copy(g, j).wait_send()
        for r in range(1, NR):
            st_copy(g, r).wait_send()
            o_copy(g, r).wait_send()
        for k in range(1, NU):
            fin_copy(g, k).wait_send()
        return carry

    lax.fori_loop(0, NG, drain, 0)


def body(queries, keys, values, block_mask, plan):
    u = lax.axis_index("uly")
    b = lax.axis_index("blk")
    mask = block_mask.reshape(NU * HL, NR, NZ, NR, NZ)
    mask = lax.dynamic_slice(mask, (u * HL, 0, b % NZ, b // NZ, 0), (HL, NR, 1, 1, NZ))
    mask = mask.reshape(HL * NR * NZ)
    bf, f32, dma = jnp.bfloat16, jnp.float32, pltpu.SemaphoreType.DMA
    any_, smem = pl.BlockSpec(memory_space=pl.ANY), pl.BlockSpec(memory_space=pltpu.SMEM)
    return pl.pallas_call(
        kernel,
        out_shape=jax.ShapeDtypeStruct(queries.shape, bf),
        in_specs=[any_, any_, any_, smem, smem],
        out_specs=pl.BlockSpec(memory_space=pltpu.VMEM),
        scratch_shapes=[
            pltpu.VMEM((NG, BT, HG * HD), bf),
            pltpu.VMEM((NG, BT, HG * HD), bf),
            pltpu.VMEM((NG, BT, HG * HD), bf),
            pltpu.VMEM((NZ, HL, BT, HD), bf),
            pltpu.VMEM((NZ, HL, HD, BT), bf),
            pltpu.VMEM((HL, NR * BT, HD), bf),
            pltpu.VMEM((HL, NZ, NR * BT), f32),
            pltpu.VMEM((HL, HD, NR * BT), f32),
            pltpu.VMEM((HL, 1, NR * BT), f32),
            pltpu.VMEM((HL, 1, NR * BT), f32),
            pltpu.VMEM((NG, NR, HG * HD, BT), bf),
            pltpu.VMEM((NG, NR, 8, BT), f32),
            pltpu.VMEM((NG, NR, HG * HD, BT), bf),
            pltpu.VMEM((NG, NR, 8, BT), f32),
            pltpu.VMEM((HL, BT, HD), bf),
            pltpu.VMEM((NU * HL, TD, HD), bf),
            dma((NG, 3, NU - 1)), dma((NG, 3, NU - 1)), dma((NG, 3)),
            dma((NG, HALF, 4)), dma((NG, HALF, 4)),
            dma((NG, 2 * NY - 1)), dma((NG, 2 * NY - 1)),
            dma((NG, NR - 1)), dma((NG, NR - 1)), dma((NG, NR - 1)), dma((NG, NR - 1)),
            dma((NG, NU - 1)), dma((NG, NU - 1)),
        ],
        compiler_params=pltpu.CompilerParams(
            collective_id=0, has_side_effects=True, vmem_limit_bytes=48 * 1024 * 1024
        ),
    )(queries, keys, values, mask, plan)


def solution(mesh):
    placed = (P(("blk", "uly"), None), P(("blk", "uly"), None), P(("blk", "uly"), None), P(), P())
    return jax.shard_map(
        body, mesh=mesh, in_specs=placed, out_specs=P(("blk", "uly"), None), check_vma=False
    )
```

time: 704 us -> 87.2 us (0.12)
  waiting for transfers between devices: 569 us -> 0 us
  Pallas kernels: 0 us -> 84.2 us
  starting transfers between devices: 53 us -> 0 us
  matrix products: 27.8 us -> 0 us
  blocking collectives: 20.9 us -> 0 us
  between operations: 13.5 us -> 0.1 us
  other arithmetic: 12.9 us -> 0 us
    all_gather x2 -> x0, waiting for transfers between devices: 557 us -> none  [the longest x1 297 us: body(): v_piece = lax.all_gather(v_head, 'blk', axis=0, tiled=True)]
    pallas_call x0 -> x1, Pallas kernels: none -> 84.2 us  [body(): pl.pallas_call(kernel, out_shape=jax.ShapeDtypeStruct(queries.shape, bf),...]
    all_to_all x2 -> x0, starting transfers between devices: 52.9 us -> none  [the longest x1 48.9 us: body(): lax.all_to_all(result, 'uly', split_axis=0, concat_axis=1, tiled=True)]
    dot_general x2 -> x0, matrix products: 27.8 us -> none  [the longest x1 14.9 us: body(): jnp.einsum('hqk,khd->hqd', expo.astype(jnp.bfloat16), v_piece, preferred_...]
    all_to_all x2 -> x0, blocking collectives: 20.9 us -> none  [the longest x1 11.7 us: body(): lax.all_to_all(k_tok, 'uly', split_axis=1, concat_axis=0, tiled=True)]
    all_to_all x2 -> x0, waiting for transfers between devices: 11.8 us -> none  [the longest x1 6.66 us: body(): lax.all_to_all(result, 'uly', split_axis=0, concat_axis=1, tiled=True)]
    reduce_sum x1 -> x0, other arithmetic: 11.5 us -> none  [body(): total = jnp.sum(expo, axis=2)]
  transfers between devices with their start and end apart: 4 -> 0, of which waited for: 4 -> 0; matrix products, arithmetic and copies ran while one was open for 4% -> 0% of each run, Pallas kernels for 0% -> 0%
where the time goes in v1:
time: 87.2 us; the launch traced here: 87.1 us
  Pallas kernels  84.2 us (97%)
  local copies, waits for them, and re-layouts  2.84 us (3%)
    pallas_call x1, Pallas kernels, body(): pl.pallas_call(kernel, out_shape=jax.ShapeDtypeStruct(queries.shape, bf),...  84.2 us
    unnamed x10, local copies, waits for them, and re-layouts  2.54 us

profile of v1, /device:TPU:1, one launch (start us, length us, event | category | flops | bytes accessed | tf_op | source)
XLA Modules:
  0.0 87.1 jit_solution(5149766583590459652)
XLA Ops:
  0.0 0.0 copy-start.3
  0.0 0.0 copy-start.2
  0.0 0.0 copy-start.1
  0.0 0.0 copy-start
  0.1 1.8 %copy.7 = s32[24,64,64]{0,2,1:T(8,128)S(1)} copy(s32[24,64,64]{2,1,0:T(8,128)} %param.8) | data formatting | bytes 786432 | tf_op args[3]
  1.9 0.1 constant_dynamic-slice_fusion
  2.0 0.1 copy.8
  2.1 0.1 reshape.7.mask_s
  2.2 0.0 copy-done.3
  2.2 0.0 copy-done.2
  2.2 0.0 copy-done.1
  2.2 0.0 copy-done
  2.3 84.2 %shard_map.55 = bf16[32,3072]{1,0:T(8,128)(2,1)S(1)} custom-call(bf16[32,3072]{1,0:T(8,128)(2,1)S(1)} %copy-done, bf16[32,3072]{1,0:T(8,128)(2,1)S(1)} %copy-done.1, bf16[32,3072]{1,0:T(8,128)(2,1)S(1)} %copy-done.2, s32[384]{0:T(512)S(1)} %reshape.7.mask_s, s32[24]{0:T(128)S(1)} %copy-done.3), custom_call_target="tpu_custom_call" | custom-call | tf_op jit(solution)/shard_map/pallas_call | solution.py:294
  86.5 0.7 copy.10
Async XLA Ops:
  0.0 2.2 %copy-start.3 = (s32[24]{0:T(128)S(1)}, s32[24]{0:T(128)}, u32[]{:S(2)}) copy-start(s32[24]{0:T(128)} %plan_s.1) | copy-start | bytes 292
  0.0 2.2 %copy-start.2 = (bf16[32,3072]{1,0:T(8,128)(2,1)S(1)}, bf16[32,3072]{1,0:T(8,128)(2,1)}, u32[]{:S(2)}) copy-start(bf16[32,3072]{1,0:T(8,128)(2,1)} %v_in.1) | copy-start | bytes 589828
  0.0 2.2 %copy-start.1 = (bf16[32,3072]{1,0:T(8,128)(2,1)S(1)}, bf16[32,3072]{1,0:T(8,128)(2,1)}, u32[]{:S(2)}) copy-start(bf16[32,3072]{1,0:T(8,128)(2,1)} %k_in.1) | copy-start | bytes 589828
  0.0 2.2 %copy-start = (bf16[32,3072]{1,0:T(8,128)(2,1)S(1)}, bf16[32,3072]{1,0:T(8,128)(2,1)}, u32[]{:S(2)}) copy-start(bf16[32,3072]{1,0:T(8,128)(2,1)} %q_in.1) | copy-start | bytes 589828

commit v2 on v0

v2 whole, which is shorter than its diff:
```python
import functools
import math

import jax
import jax.numpy as jnp
from jax import lax
from jax.experimental import pallas as pl
from jax.experimental.pallas import tpu as pltpu
from jax.sharding import PartitionSpec as P

MESH = pl.DeviceIdType.MESH
HD = 128
BT = 128
NU, NX, NY, NZ = 4, 2, 4, 8
NW = NU * NX
NB = NX * NY * NZ
HL = 3
TD = BT // NU
RUN = NX * BT
LANES = NY * RUN
HALF = NZ // 2
BIG = 1e30
NT = (((1,), (1,)), ((), ()))
RATE = math.log2(math.e) / math.sqrt(HD)
BF, F32 = jnp.bfloat16, jnp.float32


def kernel(
    q_in, k_in, v_in, mask_in, plan_s, out_ref,
    k_st, v_st, q_st, m_st, k_buf, v_buf, q_buf, shade, acc, top, tot,
    ob, st, ob_in, st_in, fin, got,
    us, ur, ul, ml, rs, rr, qs, qr, os_, or_, ss, sr, fs, fr,
):
    u = lax.axis_index("uly")
    b = lax.axis_index("blk")
    z = b % NZ
    y = (b // NZ) % NY
    x = b // (NZ * NY)
    w = u * NX + x

    def blk_at(xx, yy, zz):
        return {"blk": (xx * NY + yy % NY) * NZ + zz % NZ}

    def line_at(k):
        there = (w + k) % NW
        return {"uly": there // NX, "blk": ((there % NX) * NY + y) * NZ + z}

    up, down = blk_at(x, y, z + 1), blk_at(x, y, z + NZ - 1)
    side = [blk_at(x, y + dy, z) for dy in range(NY)]

    barrier = pltpu.get_barrier_semaphore()
    partners = [line_at(k) for k in range(1, NW)] + [up, down] + side[1:]
    for device in partners:
        pl.semaphore_signal(barrier, inc=1, device_id=device, device_id_type=MESH)

    mask_copy = pltpu.make_async_copy(mask_in.at[pl.ds(w * HL, HL)], m_st, ml)
    mask_copy.start()
    ins = ((k_in, k_st), (v_in, v_st), (q_in, q_st))
    here = pl.ds(pl.multiple_of(x * BT + u * TD, TD), TD)

    def own_in(a):
        src, dst = ins[a]
        return pltpu.make_async_copy(
            src.at[:, pl.ds(pl.multiple_of(w * HL * HD, HD), HL * HD)], dst.at[here, :], ul.at[a]
        )

    for a in range(3):
        own_in(a).start()
    pl.semaphore_wait(barrier, len(partners))

    def remote(src, dst, send, recv, device):
        return pltpu.make_async_remote_copy(
            src_ref=src, dst_ref=dst, send_sem=send, recv_sem=recv, device_id=device, device_id_type=MESH
        )

    def line_in(a, k):
        src, dst = ins[a]
        columns = pl.ds(pl.multiple_of(((w + k) % NW) * HL * HD, HD), HL * HD)
        return remote(src.at[:, columns], dst.at[here, :], us.at[a, k - 1], ur.at[a, k - 1], line_at(k))

    def ring(s, a, h, d):
        buf = (k_buf, v_buf)[a]
        src = s - 1 if d == 0 else (NZ - s + 1) % NZ
        dst = s if d == 0 else NZ - s
        i = (a * HL + h) * 2 + d
        return remote(
            buf.at[src, h], buf.at[dst, h], rs.at[s - 1, i], rr.at[s - 1, i], up if d == 0 else down
        )

    def q_copy(h, dy):
        return remote(
            q_buf.at[h, 0:RUN, :], q_buf.at[h, dy * RUN:(dy + 1) * RUN, :],
            qs.at[h, dy - 1], qr.at[h, dy - 1], side[NY - dy],
        )

    def o_copy(h, dy):
        return remote(ob.at[h, dy - 1], ob_in.at[h, dy - 1], os_.at[h, dy - 1], or_.at[h, dy - 1], side[dy])

    def st_copy(h, dy):
        return remote(st.at[h, dy - 1], st_in.at[h, dy - 1], ss.at[h, dy - 1], sr.at[h, dy - 1], side[dy])

    def fin_copy(h, k):
        there = (w + k) % NW
        rows = pl.ds(pl.multiple_of((there % NX) * BT + (there // NX) * TD, TD), TD)
        return remote(fin.at[h, rows, :], got.at[w * HL + h], fs.at[h, k - 1], fr.at[h, k - 1], line_at(k))

    def arrive(a):
        own_in(a).wait()
        for k in range(1, NW):
            line_in(a, k).wait_recv()

    def tick(s, a):
        for h in range(HL):
            for d in range(2):
                ring(s, a, h, d).wait_recv()
                last = a == d
                if last:
                    ring(s + 1, a, h, d).start()
                else:
                    @pl.when(s < HALF - 1)
                    def _():
                        ring(s + 1, a, h, d).start()

    def scores(slot, h, lo):
        return lax.dot_general(k_buf[slot, h], q_buf[h, lo:lo + BT, :], NT, preferred_element_type=F32)

    def soften(slot, h, lo, score, first):
        lanes = slice(lo, lo + BT)
        parts = [score[i * BT:(i + 1) * BT] for i in range(NX)]
        shades = [shade[h, slot * NX + i, :, lanes] for i in range(NX)]
        tops = [jnp.minimum(jnp.max(p, axis=0, keepdims=True), -m) for p, m in zip(parts, shades)]
        new_top = functools.reduce(jnp.maximum, tops)
        fade = None
        if not first:
            old_top = top[h, :, lanes]
            new_top = jnp.maximum(new_top, old_top)
            fade = jnp.exp2((old_top - new_top) * RATE)
        expo = [jnp.exp2((p - jnp.maximum(new_top, m)) * RATE) for p, m in zip(parts, shades)]
        top[h, :, lanes] = new_top
        return expo, fade

    def gather(slot, h, lo, expo, fade):
        lanes = slice(lo, lo + BT)
        weight = jnp.concatenate([e.astype(BF) for e in expo], axis=0)
        update = jnp.dot(v_buf[slot, h], weight, preferred_element_type=F32)
        total = sum(jnp.sum(e, axis=0, keepdims=True) for e in expo)
        if fade is not None:
            update = update + acc[h, :, lanes] * fade
            total = total + tot[h, :, lanes] * fade
        acc[h, :, lanes] = update
        tot[h, :, lanes] = total

    def unit(slot, heads, first=False):
        todo = [(h, lo) for h in heads for lo in range(0, LANES, BT)]
        score = scores(slot, *todo[0])
        held = None
        for i, (h, lo) in enumerate(todo):
            later = scores(slot, *todo[i + 1]) if i + 1 < len(todo) else None
            soft = soften(slot, h, lo, score, first)
            if held is not None:
                gather(slot, *todo[i - 1], *held)
            held, score = soft, later
        gather(slot, *todo[-1], *held)

    def give_back(h):
        for dy in range(1, NY):
            lanes = slice(dy * RUN, (dy + 1) * RUN)
            ob[h, dy - 1] = acc[h, :, lanes].astype(BF)
            st[h, dy - 1, 0:1, :] = top[h, :, lanes]
            st[h, dy - 1, 1:2, :] = tot[h, :, lanes]
            o_copy(h, dy).start()
            st_copy(h, dy).start()

    def combine(h):
        for dy in range(1, NY):
            o_copy(h, dy).wait_recv()
            st_copy(h, dy).wait_recv()
        own = slice(0, RUN)
        tops = [top[h, :, own]] + [st_in[h, dy, 0:1, :] for dy in range(NY - 1)]
        tots = [tot[h, :, own]] + [st_in[h, dy, 1:2, :] for dy in range(NY - 1)]
        best = functools.reduce(jnp.maximum, tops)
        fades = [jnp.exp2((t - best) * RATE) for t in tops]
        total = sum(f * t for f, t in zip(fades, tots))
        mixed = acc[h, :, own] * fades[0]
        for dy in range(NY - 1):
            mixed = mixed + ob_in[h, dy].astype(F32) * fades[dy + 1]
        fin[h] = (mixed / total).T.astype(BF)
        for k in range(1, NW):
            fin_copy(h, k).start()
        got[w * HL + h] = fin[h, here, :]

    for a in range(3):
        for k in range(1, NW):
            line_in(a, k).start()

    mask_copy.wait()
    key_row = lax.broadcasted_iota(jnp.int32, (NZ * NX, NB), 0)
    key_col = lax.broadcasted_iota(jnp.int32, (NZ * NX, NB), 1)
    key_block = ((key_row % NX) * NY + y) * NZ + (z + NZ - key_row // NX) % NZ
    pick_key = (key_col == key_block).astype(F32).astype(BF)
    run_row = lax.broadcasted_iota(jnp.int32, (NB, LANES), 0)
    run_col = lax.broadcasted_iota(jnp.int32, (NB, LANES), 1) // BT
    run_block = ((run_col % NX) * NY + (y + run_col // NX) % NY) * NZ + z
    pick_run = (run_row == run_block).astype(F32).astype(BF)
    for h in range(HL):
        allowed = (m_st[h] > 0).astype(F32).astype(BF)
        rows = lax.dot_general(pick_key, allowed, NT, preferred_element_type=F32).astype(BF)
        rows = jnp.dot(rows, pick_run, preferred_element_type=F32)
        rows = jnp.where(rows > 0.5, -BIG, BIG)
        for i in range(NZ * NX):
            shade[h, i] = rows[i:i + 1, :]

    arrive(0)
    for h in range(HL):
        k_buf[0, h] = k_st[:, h * HD:(h + 1) * HD]
        for d in range(2):
            ring(1, 0, h, d).start()
    arrive(1)
    for h in range(HL):
        v_buf[0, h] = v_st[:, h * HD:(h + 1) * HD].T
        for d in range(2):
            ring(1, 1, h, d).start()
    arrive(2)
    for h in range(HL):
        q_buf[h, 0:RUN, :] = q_st[:, h * HD:(h + 1) * HD]
        for dy in range(1, NY):
            q_copy(h, dy).start()

    heads = range(HL)

    def step(s, carry):
        tick(s, 0)

        @pl.when(s > 1)
        def _():
            unit(NZ + 1 - s, heads)

        tick(s, 1)

        @pl.when(s == 1)
        def _():
            for h in heads:
                for dy in range(1, NY):
                    q_copy(h, dy).wait_recv()
            unit(0, heads, first=True)

        unit(s, heads)
        return carry

    lax.fori_loop(1, HALF, step, 0)
    unit(HALF + 1, heads)
    for h in heads:
        ring(HALF, 0, h, 0).wait_recv()
        ring(HALF, 1, h, 1).wait_recv()
        unit(HALF, [h])
        give_back(h)

    def drain(s, carry):
        for a in range(2):
            for h in heads:
                for d in range(2):
                    ring(s, a, h, d).wait_send()
        return carry

    lax.fori_loop(1, HALF, drain, 0)
    for h in heads:
        ring(HALF, 0, h, 0).wait_send()
        ring(HALF, 1, h, 1).wait_send()
        for dy in range(1, NY):
            q_copy(h, dy).wait_send()
    for a in range(3):
        for k in range(1, NW):
            line_in(a, k).wait_send()
    for h in heads:
        combine(h)
    for h in heads:
        for dy in range(1, NY):
            o_copy(h, dy).wait_send()
            st_copy(h, dy).wait_send()
    for h in heads:
        for k in range(1, NW):
            fin_copy(h, k).wait_recv()
    for s in range(NW * HL):
        out_ref[:, s * HD:(s + 1) * HD] = got[plan_s[s]]
    for h in heads:
        for k in range(1, NW):
            fin_copy(h, k).wait_send()


def body(queries, keys, values, block_mask, plan):
    dma = pltpu.SemaphoreType.DMA
    hbm, smem = pl.BlockSpec(memory_space=pltpu.HBM), pl.BlockSpec(memory_space=pltpu.SMEM)
    return pl.pallas_call(
        kernel,
        out_shape=jax.ShapeDtypeStruct(queries.shape, BF),
        in_specs=[hbm, hbm, hbm, hbm, smem],
        out_specs=pl.BlockSpec(memory_space=pltpu.VMEM),
        scratch_shapes=[
            pltpu.VMEM((RUN, HL * HD), BF),
            pltpu.VMEM((RUN, HL * HD), BF),
            pltpu.VMEM((RUN, HL * HD), BF),
            pltpu.VMEM((HL, NB, NB), jnp.int32),
            pltpu.VMEM((NZ, HL, RUN, HD), BF),
            pltpu.VMEM((NZ, HL, HD, RUN), BF),
            pltpu.VMEM((HL, LANES, HD), BF),
            pltpu.VMEM((HL, NZ * NX, 1, LANES), F32),
            pltpu.VMEM((HL, HD, LANES), F32),
            pltpu.VMEM((HL, 1, LANES), F32),
            pltpu.VMEM((HL, 1, LANES), F32),
            pltpu.VMEM((HL, NY - 1, HD, RUN), BF),
            pltpu.VMEM((HL, NY - 1, 8, RUN), F32),
            pltpu.VMEM((HL, NY - 1, HD, RUN), BF),
            pltpu.VMEM((HL, NY - 1, 8, RUN), F32),
            pltpu.VMEM((HL, RUN, HD), BF),
            pltpu.VMEM((NW * HL, TD, HD), BF),
            dma((3, NW - 1)), dma((3, NW - 1)), dma((3,)), dma,
            dma((HALF, 4 * HL)), dma((HALF, 4 * HL)),
            dma((HL, NY - 1)), dma((HL, NY - 1)),
            dma((HL, NY - 1)), dma((HL, NY - 1)), dma((HL, NY - 1)), dma((HL, NY - 1)),
            dma((HL, NW - 1)), dma((HL, NW - 1)),
        ],
        compiler_params=pltpu.CompilerParams(
            collective_id=0, has_side_effects=True, vmem_limit_bytes=48 * 1024 * 1024
        ),
    )(queries, keys, values, block_mask, plan)


def solution(mesh):
    placed = (P(("blk", "uly"), None), P(("blk", "uly"), None), P(("blk", "uly"), None), P(), P())
    return jax.shard_map(
        body, mesh=mesh, in_specs=placed, out_specs=P(("blk", "uly"), None), check_vma=False
    )
```

time: 704 us -> 70.2 us (0.10)
  waiting for transfers between devices: 569 us -> 0 us
  Pallas kernels: 0 us -> 64.7 us
  starting transfers between devices: 53 us -> 0 us
  matrix products: 27.8 us -> 0 us
  blocking collectives: 20.9 us -> 0 us
  between operations: 13.5 us -> 0.01 us
  other arithmetic: 12.9 us -> 0 us
    all_gather x2 -> x0, waiting for transfers between devices: 557 us -> none  [the longest x1 297 us: body(): v_piece = lax.all_gather(v_head, 'blk', axis=0, tiled=True)]
    pallas_call x0 -> x1, Pallas kernels: none -> 64.7 us  [body(): pl.pallas_call(kernel, out_shape=jax.ShapeDtypeStruct(queries.shape, BF),...]
    all_to_all x2 -> x0, starting transfers between devices: 52.9 us -> none  [the longest x1 48.9 us: body(): lax.all_to_all(result, 'uly', split_axis=0, concat_axis=1, tiled=True)]
    dot_general x2 -> x0, matrix products: 27.8 us -> none  [the longest x1 14.9 us: body(): jnp.einsum('hqk,khd->hqd', expo.astype(jnp.bfloat16), v_piece, preferred_...]
    all_to_all x2 -> x0, blocking collectives: 20.9 us -> none  [the longest x1 11.7 us: body(): lax.all_to_all(k_tok, 'uly', split_axis=1, concat_axis=0, tiled=True)]
    all_to_all x2 -> x0, waiting for transfers between devices: 11.8 us -> none  [the longest x1 6.66 us: body(): lax.all_to_all(result, 'uly', split_axis=0, concat_axis=1, tiled=True)]
    reduce_sum x1 -> x0, other arithmetic: 11.5 us -> none  [body(): total = jnp.sum(expo, axis=2)]
  transfers between devices with their start and end apart: 4 -> 0, of which waited for: 4 -> 0; matrix products, arithmetic and copies ran while one was open for 4% -> 0% of each run, Pallas kernels for 0% -> 0%
where the time goes in v2:
time: 70.2 us; the launch traced here: 70 us
  Pallas kernels  64.7 us (92%)
  local copies, waits for them, and re-layouts  5.25 us (7%)
    pallas_call x1, Pallas kernels, body(): pl.pallas_call(kernel, out_shape=jax.ShapeDtypeStruct(queries.shape, BF),...  64.7 us
    unnamed x11, local copies, waits for them, and re-layouts  5.25 us

profile of v2, /device:TPU:1, one launch (start us, length us, event | category | flops | bytes accessed | tf_op | source)
XLA Modules:
  0.0 70.0 jit_solution(15181079384307473433)
XLA Ops:
  0.0 0.0 copy-start
  0.0 1.1 %copy-done = s32[24,64,64]{2,1,0:T(8,128)S(1)} copy-done((s32[24,64,64]{2,1,0:T(8,128)S(1)}, s32[24,64,64]{2,1,0:T(8,128)}, u32[]{:S(2)}) %copy-start) | copy-done | bytes 393240
  1.1 0.0 copy-start.1
  1.1 0.9 %copy-done.1 = bf16[32,3072]{1,0:T(8,128)(2,1)S(1)} copy-done((bf16[32,3072]{1,0:T(8,128)(2,1)S(1)}, bf16[32,3072]{1,0:T(8,128)(2,1)}, u32[]{:S(2)}) %copy-start.1) | copy-done | bytes 196632
  2.1 0.0 copy-start.2
  2.1 0.9 %copy-done.2 = bf16[32,3072]{1,0:T(8,128)(2,1)S(1)} copy-done((bf16[32,3072]{1,0:T(8,128)(2,1)S(1)}, bf16[32,3072]{1,0:T(8,128)(2,1)}, u32[]{:S(2)}) %copy-start.2) | copy-done | bytes 196632
  3.0 0.0 copy-start.3
  3.0 0.9 %copy-done.3 = bf16[32,3072]{1,0:T(8,128)(2,1)S(1)} copy-done((bf16[32,3072]{1,0:T(8,128)(2,1)S(1)}, bf16[32,3072]{1,0:T(8,128)(2,1)}, u32[]{:S(2)}) %copy-start.3) | copy-done | bytes 196632
  3.9 0.0 copy-start.4
  3.9 0.7 copy-done.4
  4.6 64.7 %shard_map.55 = bf16[32,3072]{1,0:T(8,128)(2,1)S(1)} custom-call(bf16[32,3072]{1,0:T(8,128)(2,1)S(1)} %copy-done.1, bf16[32,3072]{1,0:T(8,128)(2,1)S(1)} %copy-done.2, bf16[32,3072]{1,0:T(8,128)(2,1)S(1)} %copy-done.3, s32[24,64,64]{2,1,0:T(8,128)S(1)} %copy-done, s32[24]{0:T(128)S(1)} %copy-done.4), custom_call_target="tpu_custom_call" | custom-call | tf_op jit(solution)/shard_map/pallas_call | solution.py:293
  69.3 0.7 copy.7
Async XLA Ops:
  0.0 1.1 %copy-start = (s32[24,64,64]{2,1,0:T(8,128)S(1)}, s32[24,64,64]{2,1,0:T(8,128)}, u32[]{:S(2)}) copy-start(s32[24,64,64]{2,1,0:T(8,128)} %mask_in.1) | copy-start | bytes 1179652
  1.1 0.9 %copy-start.1 = (bf16[32,3072]{1,0:T(8,128)(2,1)S(1)}, bf16[32,3072]{1,0:T(8,128)(2,1)}, u32[]{:S(2)}) copy-start(bf16[32,3072]{1,0:T(8,128)(2,1)} %q_in.1) | copy-start | bytes 589828
  2.1 0.9 %copy-start.2 = (bf16[32,3072]{1,0:T(8,128)(2,1)S(1)}, bf16[32,3072]{1,0:T(8,128)(2,1)}, u32[]{:S(2)}) copy-start(bf16[32,3072]{1,0:T(8,128)(2,1)} %k_in.1) | copy-start | bytes 589828
  3.0 0.9 %copy-start.3 = (bf16[32,3072]{1,0:T(8,128)(2,1)S(1)}, bf16[32,3072]{1,0:T(8,128)(2,1)}, u32[]{:S(2)}) copy-start(bf16[32,3072]{1,0:T(8,128)(2,1)} %v_in.1) | copy-start | bytes 589828
  3.9 0.7 copy-start.4

commit v3 on v2

v3 whole, which is shorter than its diff:
```python
import functools
import math

import jax
import jax.numpy as jnp
from jax import lax
from jax.experimental import pallas as pl
from jax.experimental.pallas import tpu as pltpu
from jax.sharding import PartitionSpec as P

MESH = pl.DeviceIdType.MESH
HD = 128
BT = 128
NU, NX, NY, NZ = 4, 2, 4, 8
NW = NU * NX
NB = NX * NY * NZ
HL = 3
TD = BT // NU
RUN = NX * BT
LANES = NY * RUN
HALF = NZ // 2
BIG = 1e30
VMEM_MIB = 62
NT = (((1,), (1,)), ((), ()))
RATE = math.log2(math.e) / math.sqrt(HD)
BF, F32 = jnp.bfloat16, jnp.float32


def kernel(
    q_in, k_in, v_in, mask_in, plan_s, out_ref,
    kv, v_st, q_buf, m_st, shade, acc, top, tot, ob, ob_in, fin, got,
    us, ur, ul, ml, rs, rr, qs, qr, os_, or_, fs, fr,
):
    u = lax.axis_index("uly")
    b = lax.axis_index("blk")
    z = b % NZ
    y = (b // NZ) % NY
    x = b // (NZ * NY)
    w = u * NX + x
    heads = range(HL)

    def blk_at(yy, zz):
        return {"blk": (x * NY + yy % NY) * NZ + zz % NZ}

    def line_at(k):
        there = (w + k) % NW
        return {"uly": there // NX, "blk": ((there % NX) * NY + y) * NZ + z}

    up, down = blk_at(y, z + 1), blk_at(y, z + NZ - 1)
    side = [blk_at(y + dy, z) for dy in range(NY)]

    barrier = pltpu.get_barrier_semaphore()
    partners = [line_at(k) for k in range(1, NW)] + [up, down] + side[1:]
    for device in partners:
        pl.semaphore_signal(barrier, inc=1, device_id=device, device_id_type=MESH)

    mask_copy = pltpu.make_async_copy(mask_in.at[pl.ds(w * HL, HL)], m_st, ml)
    mask_copy.start()
    ins = ((k_in, kv.at[0]), (v_in, v_st), (q_in, q_buf))
    here = pl.ds(pl.multiple_of(x * BT + u * TD, TD), TD)

    def columns_of(there, h):
        return pl.ds(pl.multiple_of((there * HL + h) * HD, HD), HD)

    def own_in(a, h):
        src, dst = ins[a]
        return pltpu.make_async_copy(src.at[:, columns_of(w, h)], dst.at[h, here, :], ul.at[a, h])

    for a in range(3):
        for h in heads:
            own_in(a, h).start()
    pl.semaphore_wait(barrier, len(partners))

    def remote(src, dst, send, recv, device):
        return pltpu.make_async_remote_copy(
            src_ref=src, dst_ref=dst, send_sem=send, recv_sem=recv, device_id=device, device_id_type=MESH
        )

    def sum_of(ref, send, recv):
        return remote(ref, ref, send, recv, up)

    def line_in(a, h, k):
        src, dst = ins[a]
        return remote(
            src.at[:, columns_of((w + k) % NW, h)], dst.at[h, here, :], us.at[a, h], ur.at[a, h], line_at(k)
        )

    def line_all(a, h):
        return sum_of(v_st.at[h, 0:(NW - 1) * TD, :], us.at[a, h], ur.at[a, h])

    def ring(s, h, d):
        src = s - 1 if d == 0 else (NZ - s + 1) % NZ
        dst = s if d == 0 else NZ - s
        return remote(
            kv.at[src, h], kv.at[dst, h], rs.at[s - 1], rr.at[s - 1, h, d], up if d == 0 else down
        )

    def ring_last(h, d):
        rows = slice(d * RUN, (d + 1) * RUN)
        src = HALF - 1 if d == 0 else HALF + 1
        return remote(
            kv.at[src, h, rows, :], kv.at[HALF, h, rows, :],
            rs.at[HALF - 1], rr.at[HALF - 1, h, d], up if d == 0 else down,
        )

    def q_copy(h, dy):
        return remote(
            q_buf.at[h, 0:RUN, :], q_buf.at[h, dy * RUN:(dy + 1) * RUN, :], qs.at[h], qr.at[h], side[NY - dy]
        )

    def q_all(h):
        return sum_of(q_buf.at[h, RUN:NY * RUN, :], qs.at[h], qr.at[h])

    def o_copy(h, dy):
        return remote(ob.at[h, dy - 1], ob_in.at[h, dy - 1], os_.at[h], or_.at[h], side[dy])

    def o_all(h):
        return sum_of(ob_in.at[h], os_.at[h], or_.at[h])

    def fin_copy(h, k):
        there = (w + k) % NW
        rows = pl.ds(pl.multiple_of((there % NX) * BT + (there // NX) * TD, TD), TD)
        return remote(fin.at[h, rows, :], got.at[w * HL + h], fs.at[h], fr.at[h], line_at(k))

    def fin_all(h):
        return sum_of(got.at[0:NW - 1], fs.at[h], fr.at[h])

    def arrive(a, h):
        own_in(a, h).wait()
        line_all(a, h).wait_recv()

    def scores(slot, h, lo):
        return lax.dot_general(kv[slot, h, 0:RUN, :], q_buf[h, lo:lo + BT, :], NT, preferred_element_type=F32)

    def soften(slot, h, lo, score, first):
        lanes = slice(lo, lo + BT)
        parts = [score[i * BT:(i + 1) * BT] for i in range(NX)]
        shades = [shade[h, slot * NX + i, :, lanes] for i in range(NX)]
        tops = [jnp.minimum(jnp.max(p, axis=0, keepdims=True), -m) for p, m in zip(parts, shades)]
        new_top = functools.reduce(jnp.maximum, tops)
        fade = None
        if not first:
            old_top = top[h, :, lanes]
            new_top = jnp.maximum(new_top, old_top)
            fade = jnp.exp2((old_top - new_top) * RATE)
        expo = [jnp.exp2((p - jnp.maximum(new_top, m)) * RATE) for p, m in zip(parts, shades)]
        top[h, :, lanes] = new_top
        return expo, fade

    def gather(slot, h, lo, expo, fade):
        lanes = slice(lo, lo + BT)
        vals = jnp.concatenate([kv[slot, h, RUN + i * BT:RUN + (i + 1) * BT, :] for i in range(NX)], axis=1)
        weight = jnp.concatenate([e.astype(BF) for e in expo], axis=0)
        update = jnp.dot(vals, weight, preferred_element_type=F32)
        total = sum(jnp.sum(e, axis=0, keepdims=True) for e in expo)
        if fade is not None:
            update = update + acc[h, :, lanes] * fade
            total = total + tot[h, :, lanes] * fade
        acc[h, :, lanes] = update
        tot[h, :, lanes] = total

    def unit(pairs, first=False):
        todo = [(slot, h, lo) for slot, h in pairs for lo in range(0, LANES, BT)]
        score = scores(*todo[0])
        held = None
        for i, item in enumerate(todo):
            later = scores(*todo[i + 1]) if i + 1 < len(todo) else None
            soft = soften(*item, score, first)
            if held is not None:
                gather(*todo[i - 1], *held)
            held, score = soft, later
        gather(*todo[-1], *held)

    def split3(value):
        terms = []
        for _ in range(3):
            term = value.astype(BF).astype(F32)
            terms.append(term)
            value = value - term
        return terms

    def give_back(h):
        row = lax.broadcasted_iota(jnp.int32, (16, RUN), 0)
        for dy in range(1, NY):
            lanes = slice(dy * RUN, (dy + 1) * RUN)
            ob[h, dy - 1, 0:HD, :] = acc[h, :, lanes].astype(BF)
            notes = jnp.zeros((16, RUN), F32)
            for i, term in enumerate(split3(top[h, :, lanes]) + split3(tot[h, :, lanes])):
                notes = jnp.where(row == i, term, notes)
            ob[h, dy - 1, HD:HD + 16, :] = notes.astype(BF)
            o_copy(h, dy).start()

    def combine(h):
        o_all(h).wait_recv()
        own = slice(0, RUN)
        notes = [ob_in[h, dy, HD:HD + 16, :].astype(F32) for dy in range(NY - 1)]
        tops = [top[h, :, own]] + [n[0:1] + n[1:2] + n[2:3] for n in notes]
        tots = [tot[h, :, own]] + [n[3:4] + n[4:5] + n[5:6] for n in notes]
        best = functools.reduce(jnp.maximum, tops)
        fades = [jnp.exp2((t - best) * RATE) for t in tops]
        share = 1.0 / sum(f * t for f, t in zip(fades, tots))
        mixed = acc[h, :, own] * (fades[0] * share)
        for dy in range(NY - 1):
            mixed = mixed + ob_in[h, dy, 0:HD, :].astype(F32) * (fades[dy + 1] * share)
        fin[h] = mixed.astype(BF).T
        for k in range(1, NW):
            fin_copy(h, k).start()
        got[w * HL + h] = fin[h, here, :]

    for h in heads:
        for a in range(2):
            for k in range(1, NW):
                line_in(a, h, k).start()
    for h in heads:
        for k in range(1, NW):
            line_in(2, h, k).start()

    for h in heads:
        arrive(0, h)
        arrive(1, h)
        for i in range(NX):
            kv[0, h, RUN + i * BT:RUN + (i + 1) * BT, :] = v_st[h, i * BT:(i + 1) * BT, :].T
        for d in range(2):
            ring(1, h, d).start()
    for h in heads:
        arrive(2, h)
        for dy in range(1, NY):
            q_copy(h, dy).start()

    mask_copy.wait()
    key_row = lax.broadcasted_iota(jnp.int32, (NZ * NX, NB), 0)
    key_col = lax.broadcasted_iota(jnp.int32, (NZ * NX, NB), 1)
    key_block = ((key_row % NX) * NY + y) * NZ + (z + NZ - key_row // NX) % NZ
    pick_key = (key_col == key_block).astype(F32).astype(BF)
    run_row = lax.broadcasted_iota(jnp.int32, (NB, LANES), 0)
    run_col = lax.broadcasted_iota(jnp.int32, (NB, LANES), 1) // BT
    run_block = ((run_col % NX) * NY + (y + run_col // NX) % NY) * NZ + z
    pick_run = (run_row == run_block).astype(F32).astype(BF)
    for h in heads:
        allowed = (m_st[h] > 0).astype(F32).astype(BF)
        rows = lax.dot_general(pick_key, allowed, NT, preferred_element_type=F32).astype(BF)
        rows = jnp.dot(rows, pick_run, preferred_element_type=F32)
        rows = jnp.where(rows > 0.5, -BIG, BIG)
        for i in range(NZ * NX):
            shade[h, i] = rows[i:i + 1, :]

    def tick(s, h):
        ring(s, h, 0).wait_recv()
        ring(s, h, 1).wait_recv()

    def forward(s, h):
        ring(s, h, 0).start()
        ring(s, h, 1).start()

    def step(s, carry):
        tick(s, 0)
        forward(s + 1, 0)

        @pl.when(s > 1)
        def _():
            unit([(s - 1, h) for h in heads])

        tick(s, 1)
        forward(s + 1, 1)

        @pl.when(s > 1)
        def _():
            unit([(NZ + 1 - s, h) for h in heads])

        tick(s, 2)

        @pl.when(s == 1)
        def _():
            forward(s + 1, 2)
            for h in heads:
                q_all(h).wait_recv()
            unit([(0, h) for h in heads], first=True)

        return carry

    lax.fori_loop(1, HALF - 1, step, 0)

    def finish(h):
        unit([(HALF - 1, h), (HALF + 1, h)])
        for d in range(2):
            ring_last(h, d).wait_recv()
        unit([(HALF, h)])
        give_back(h)

    def last(h):
        for d in range(2):
            ring_last(h, d).start()

    tick(HALF - 1, 0)
    last(0)
    forward(HALF - 1, 2)
    unit([(HALF - 2, h) for h in heads])
    tick(HALF - 1, 1)
    last(1)
    unit([(HALF + 2, h) for h in heads])
    finish(0)
    tick(HALF - 1, 2)
    last(2)
    finish(1)
    combine(0)
    finish(2)
    for s in range(1, HALF):
        sum_of(kv.at[0:2], rs.at[s - 1], rr.at[s - 1, 0, 0]).wait_send()
    sum_of(kv.at[0], rs.at[HALF - 1], rr.at[HALF - 1, 0, 0]).wait_send()
    for h in heads:
        q_all(h).wait_send()
        for a in range(3):
            line_all(a, h).wait_send()
    combine(1)
    combine(2)
    for h in heads:
        o_all(h).wait_send()
    for h in heads:
        fin_all(h).wait_recv()
    for s in range(NW * HL):
        out_ref[:, s * HD:(s + 1) * HD] = got[plan_s[s]]
    for h in heads:
        fin_all(h).wait_send()


def body(queries, keys, values, block_mask, plan):
    dma = pltpu.SemaphoreType.DMA
    hbm, smem = pl.BlockSpec(memory_space=pl.ANY), pl.BlockSpec(memory_space=pltpu.SMEM)
    return pl.pallas_call(
        kernel,
        out_shape=jax.ShapeDtypeStruct(queries.shape, BF),
        in_specs=[hbm, hbm, hbm, hbm, smem],
        out_specs=pl.BlockSpec(memory_space=pltpu.VMEM),
        scratch_shapes=[
            pltpu.VMEM((NZ, HL, 2 * RUN, HD), BF),
            pltpu.VMEM((HL, RUN, HD), BF),
            pltpu.VMEM((HL, LANES, HD), BF),
            pltpu.VMEM((HL, NB, NB), jnp.int32),
            pltpu.VMEM((HL, NZ * NX, 1, LANES), F32),
            pltpu.VMEM((HL, HD, LANES), F32),
            pltpu.VMEM((HL, 1, LANES), F32),
            pltpu.VMEM((HL, 1, LANES), F32),
            pltpu.VMEM((HL, NY - 1, HD + 16, RUN), BF),
            pltpu.VMEM((HL, NY - 1, HD + 16, RUN), BF),
            pltpu.VMEM((HL, RUN, HD), BF),
            pltpu.VMEM((NW * HL, TD, HD), BF),
            dma((3, HL)), dma((3, HL)), dma((3, HL)), dma,
            dma((HALF,)), dma((HALF, HL, 2)),
            dma((HL,)), dma((HL,)),
            dma((HL,)), dma((HL,)),
            dma((HL,)), dma((HL,)),
        ],
        compiler_params=pltpu.CompilerParams(
            collective_id=0, has_side_effects=True, vmem_limit_bytes=VMEM_MIB * 1024 * 1024
        ),
    )(queries, keys, values, block_mask, plan)


def solution(mesh):
    placed = (P(("blk", "uly"), None), P(("blk", "uly"), None), P(("blk", "uly"), None), P(), P())
    return jax.shard_map(
        body, mesh=mesh, in_specs=placed, out_specs=P(("blk", "uly"), None), check_vma=False
    )
```

time: 70.2 us -> 62.2 us (0.89)
  Pallas kernels: 64.7 us -> 60.5 us
  local copies, waits for them, and re-layouts: 5.25 us -> 1.62 us
    pallas_call x1, Pallas kernels: 64.7 us -> 60.5 us  [body(): pl.pallas_call(kernel, out_shape=jax.ShapeDtypeStruct(queries.shape, BF),...]
    unnamed x11 -> x1, local copies, waits for them, and re-layouts: 5.25 us -> 1.62 us
where the time goes in v3:
time: 62.2 us; the launch traced here: 62.1 us
  Pallas kernels  60.5 us (97%)
  local copies, waits for them, and re-layouts  1.62 us (3%)
    pallas_call x1, Pallas kernels, body(): pl.pallas_call(kernel, out_shape=jax.ShapeDtypeStruct(queries.shape, BF),...  60.5 us
    unnamed x1, local copies, waits for them, and re-layouts  1.62 us

profile of v3, /device:TPU:1, one launch (start us, length us, event | category | flops | bytes accessed | tf_op | source)
XLA Modules:
  0.0 62.1 jit_solution(3747509185151593498)
XLA Ops:
  0.0 60.5 %shard_map.55 = bf16[32,3072]{1,0:T(8,128)(2,1)} custom-call(bf16[32,3072]{1,0:T(8,128)(2,1)} %q_in.1, bf16[32,3072]{1,0:T(8,128)(2,1)} %k_in.1, bf16[32,3072]{1,0:T(8,128)(2,1)} %v_in.1, s32[24,64,64]{2,1,0:T(8,128)} %mask_in.1, s32[24]{0:T(128)} %plan_s.1), custom_call_target="tpu_custom_call" | custom-call | tf_op jit(solution)/shard_map/pallas_call | solution.py:329
  60.5 1.6 %copy.7 = bf16[32,3072]{1,0:T(8,128)(2,1)} copy(bf16[32,3072]{1,0:T(8,128)(2,1)} %shard_map.55) | data formatting | bytes 393216

commit v4 on v0

v4 whole, which is shorter than its diff:
```python
import functools
import math

import jax
import jax.numpy as jnp
from jax import lax
from jax.experimental import pallas as pl
from jax.experimental.pallas import tpu as pltpu
from jax.sharding import PartitionSpec as P

MESH = pl.DeviceIdType.MESH
H, HD, BT, TD = 24, 128, 128, 32
NX, NY, NZ = 4, 4, 8
NB = 64
HL = H // NZ
SETS = 3
RUN = NZ * TD
LANES = NX * RUN
BIG, FLOOR = 1e30, -1e29
VMEM_MIB = 62
NT = (((1,), (1,)), ((), ()))
RATE = math.log2(math.e) / math.sqrt(HD)
BF, F32 = jnp.bfloat16, jnp.float32
K, V, Q = 0, 1, 2


def kernel(
    q_in, k_in, v_in, mask_in, plan_s, out_ref,
    kb, vb, v_st, q_buf, m_st, shade, acc, top, tot, ob, ob_in, fin, got,
    us, ur, ul, ml, ys, yr, cs, cr, qs, qr, os_, or_, fs, fr,
):
    u = lax.axis_index("uly")
    b = lax.axis_index("blk")
    core = u % 2
    z = b % NZ
    y = (b // NZ) % NY
    x = (u // 2) * 2 + b // (NZ * NY)

    def at(xx, yy, zz, cc):
        xx, yy, zz = xx % NX, yy % NY, zz % NZ
        return {"uly": (xx // 2) * 2 + cc, "blk": ((xx % 2) * NY + yy) * NZ + zz}

    same = [at(x, y, z + k, core) for k in range(NZ)]
    cross = [at(x, y, z + k, 1 - core) for k in range(NZ)]
    y_side = [at(x, y + d, z, core) for d in range(NY)]
    x_side = [at(x + d, y, z, core) for d in range(NX)]

    barrier = pltpu.get_barrier_semaphore()
    partners = same[1:] + cross + y_side[1:] + x_side[1:]
    for device in partners:
        pl.semaphore_signal(barrier, inc=1, device_id=device, device_id_type=MESH)

    mask_copy = pltpu.make_async_copy(mask_in.at[pl.ds(z * HL, HL)], m_st, ml)
    mask_copy.start()
    here = pl.ds(pl.multiple_of(z * TD, TD), TD)
    sources = (k_in, v_in, q_in)

    def place(a, i):
        if a == V:
            return v_st.at[i, here, :]
        if a == Q:
            return q_buf.at[i, here, :]
        return kb.at[i // 2, 0, i % 2, here, :]

    def columns_of(i, k):
        there = (z + k) % NZ
        lead = (2 * core, 2 - 2 * core, 1)[i]
        return pl.ds(pl.multiple_of((there * HL + lead) * HD, HD), HD)

    def own_in(a, i):
        return pltpu.make_async_copy(sources[a].at[:, columns_of(i, 0)], place(a, i), ul.at[a, i])

    for a in range(3):
        for i in (2, 0):
            own_in(a, i).start()
    pl.semaphore_wait(barrier, len(partners))

    def remote(src, dst, send, recv, device):
        return pltpu.make_async_remote_copy(
            src_ref=src, dst_ref=dst, send_sem=send, recv_sem=recv, device_id=device, device_id_type=MESH
        )

    def sum_of(ref, send, recv):
        return remote(ref, ref, send, recv, same[1])

    def first_of(i):
        return 0 if i == 1 else 1

    def entry(a, i, k):
        device = cross[k] if i == 1 else same[k]
        return remote(sources[a].at[:, columns_of(i, k)], place(a, i), us.at[a, i], ur.at[a, i], device)

    def entry_all(a, i):
        return sum_of(v_st.at[i, 0:(NZ - first_of(i)) * TD, :], us.at[a, i], ur.at[a, i])

    def send_in(a, i):
        for k in range(first_of(i), NZ):
            entry(a, i, k).start()

    def arrive(a, i):
        if i != 1:
            own_in(a, i).wait()
        entry_all(a, i).wait_recv()

    def y_copy(hk, a, d):
        buf = vb if a == V else kb
        src, dst = (buf.at[0, 0], buf.at[0, d]) if hk == 0 else (buf.at[1, 0, 0], buf.at[1, d, 0])
        return remote(src, dst, ys.at[hk, a], yr.at[hk, a, d - 1], y_side[NY - d])

    def y_all(hk, a):
        ref = kb.at[0, 1:NY] if hk == 0 else kb.at[1, 1:NY, 0]
        return sum_of(ref, ys.at[hk, a], yr.at[hk, a, 0])

    def c_copy(a, d):
        buf = vb if a == V else kb
        return remote(buf.at[1, d, 0], buf.at[1, d, 1], cs.at[a], cr.at[a, d], cross[0])

    def c_all(a):
        return sum_of(kb.at[1, 0:NY, 0], cs.at[a], cr.at[a, 0])

    def q_copy(i, d):
        return remote(
            q_buf.at[i, 0:RUN, :], q_buf.at[i, d * RUN:(d + 1) * RUN, :], qs.at[i], qr.at[i], x_side[NX - d]
        )

    def q_all(i):
        return sum_of(q_buf.at[i, RUN:LANES, :], qs.at[i], qr.at[i])

    def o_copy(i, d):
        return remote(ob.at[i, d - 1], ob_in.at[i, d - 1], os_.at[i], or_.at[i], x_side[d])

    def o_all(i):
        return sum_of(ob_in.at[i], os_.at[i], or_.at[i])

    mine = (z * HL + 2 * core, z * HL + 2 * core, z * HL + 1)

    def fin_copy(i, k):
        rows = pl.ds(pl.multiple_of(((z + k) % NZ) * TD, TD), TD)
        device = cross[k] if i == 1 else same[k]
        return remote(fin.at[i, rows, :], got.at[mine[i]], fs.at[i], fr.at[i], device)

    def fin_all(i):
        return sum_of(got.at[0:NZ - first_of(i)], fs.at[i], fr.at[i])

    def turn(i):
        for n in range(RUN // HD):
            rows = slice(n * HD, (n + 1) * HD)
            vb[i // 2, 0, i % 2, rows, :] = v_st[i, rows, :].T

    def scores(d, half, i, lo):
        return lax.dot_general(kb[i // 2, d, half], q_buf[i, lo:lo + BT, :], NT, preferred_element_type=F32)

    def soften(d, half, i, lo, score, first):
        lanes = slice(lo, lo + BT)
        bias = shade[i // 2, d, :, lanes]
        parts = [score[n * TD:(n + 1) * TD] for n in range(NZ)]
        tops = [jnp.max(p.reshape(TD // 8, 8, BT), axis=0) + bias[n:n + 1] for n, p in enumerate(parts)]
        new_top = jnp.maximum(jnp.max(functools.reduce(jnp.maximum, tops), axis=0, keepdims=True), FLOOR)
        fade = None
        if not first:
            old_top = top[i, :, lanes]
            new_top = jnp.maximum(new_top, old_top)
            fade = jnp.exp2((old_top - new_top) * RATE)
        shift = (bias - new_top) * RATE
        expo = [jnp.exp2(p * RATE + shift[n:n + 1]) for n, p in enumerate(parts)]
        top[i, :, lanes] = new_top
        return jnp.concatenate(expo, axis=0), fade

    def gather(d, half, i, lo, expo, fade):
        lanes = slice(lo, lo + BT)
        vals = jnp.concatenate([vb[i // 2, d, half, n * HD:(n + 1) * HD, :] for n in range(RUN // HD)], axis=1)
        update = jnp.dot(vals, expo.astype(BF), preferred_element_type=F32)
        total = jnp.sum(expo, axis=0, keepdims=True)
        if fade is not None:
            update = update + acc[i, :, lanes] * fade
            total = total + tot[i, :, lanes] * fade
        acc[i, :, lanes] = update
        tot[i, :, lanes] = total

    def unit(parts, first=False):
        todo = [(d, half, i, lo) for d, half, i in parts for lo in range(0, LANES, BT)]
        fresh = len(parts) if first is True else first
        score = scores(*todo[0])
        held = None
        for n, item in enumerate(todo):
            later = scores(*todo[n + 1]) if n + 1 < len(todo) else None
            soft = soften(*item, score, n < fresh * (LANES // BT))
            if held is not None:
                gather(*todo[n - 1], *held)
            held, score = soft, later
        gather(*todo[-1], *held)

    def split3(value):
        terms = []
        for _ in range(3):
            term = value.astype(BF).astype(F32)
            terms.append(term)
            value = value - term
        return terms

    def give_back(i):
        row = lax.broadcasted_iota(jnp.int32, (16, RUN), 0)
        for d in range(1, NX):
            lanes = slice(d * RUN, (d + 1) * RUN)
            ob[i, d - 1, 0:HD, :] = acc[i, :, lanes].astype(BF)
            notes = jnp.zeros((16, RUN), F32)
            for n, term in enumerate(split3(top[i, :, lanes]) + split3(tot[i, :, lanes])):
                notes = jnp.where(row == n, term, notes)
            ob[i, d - 1, HD:HD + 16, :] = notes.astype(BF)
            o_copy(i, d).start()

    def combine(i):
        o_all(i).wait_recv()
        own = slice(0, RUN)
        notes = [ob_in[i, d, HD:HD + 16, :].astype(F32) for d in range(NX - 1)]
        tops = [top[i, :, own]] + [n[0:1] + n[1:2] + n[2:3] for n in notes]
        tots = [tot[i, :, own]] + [n[3:4] + n[4:5] + n[5:6] for n in notes]
        best = functools.reduce(jnp.maximum, tops)
        fades = [jnp.exp2((t - best) * RATE) for t in tops]
        share = 1.0 / sum(f * t for f, t in zip(fades, tots))
        mixed = acc[i, :, own] * (fades[0] * share)
        for d in range(NX - 1):
            mixed = mixed + ob_in[i, d, 0:HD, :].astype(F32) * (fades[d + 1] * share)
        fin[i] = mixed.astype(BF).T
        for k in range(first_of(i), NZ):
            fin_copy(i, k).start()
        if i != 1:
            got[mine[i]] = fin[i, here, :]

    for a in (K, V, Q):
        send_in(a, 2)
    for a in (K, Q, V):
        send_in(a, 0)
        send_in(a, 1)

    arrive(K, 2)
    for d in range(1, NY):
        y_copy(1, K, d).start()
    c_copy(K, 0).start()
    arrive(V, 2)
    turn(2)
    for d in range(1, NY):
        y_copy(1, V, d).start()
    c_copy(V, 0).start()
    arrive(Q, 2)
    for d in range(1, NX):
        q_copy(2, d).start()

    mask_copy.wait()
    key_row = lax.broadcasted_iota(jnp.int32, (NY * NZ, NB), 0)
    key_col = lax.broadcasted_iota(jnp.int32, (NY * NZ, NB), 1)
    key_block = ((x % 2) * NY + (y + key_row // NZ) % NY) * NZ + key_row % NZ
    pick_key = (key_col == key_block).astype(F32).astype(BF)
    run_row = lax.broadcasted_iota(jnp.int32, (NB, LANES), 0)
    run_col = lax.broadcasted_iota(jnp.int32, (NB, LANES), 1)
    run_block = (((x + run_col // RUN) % 2) * NY + y) * NZ + (run_col // TD) % NZ
    pick_run = (run_row == run_block).astype(F32).astype(BF)
    for hk in range(2):
        allowed = (m_st[2 * core if hk == 0 else 1] > 0).astype(F32).astype(BF)
        rows = lax.dot_general(pick_key, allowed, NT, preferred_element_type=F32).astype(BF)
        rows = jnp.dot(rows, pick_run, preferred_element_type=F32)
        rows = jnp.where(rows > 0.5, 0.0, -BIG)
        for d in range(NY):
            shade[hk, d] = rows[d * NZ:(d + 1) * NZ, :]

    for i in (0, 1):
        arrive(K, i)
    for d in range(1, NY):
        y_copy(0, K, d).start()
    for i in (0, 1):
        arrive(Q, i)
        for d in range(1, NX):
            q_copy(i, d).start()
    for i in (0, 1):
        arrive(V, i)
        turn(i)
    for d in range(1, NY):
        y_copy(0, V, d).start()

    for d in (1, 3, 2):
        for a in (K, V):
            y_copy(1, a, d).wait_recv()
            c_copy(a, d).start()
    q_all(2).wait_recv()
    unit([(d, 0, 2) for d in (0, 1, 3, 2)], first=1)
    for d in range(NY):
        for a in (K, V):
            c_copy(a, d).wait_recv()
    unit([(d, 1, 2) for d in range(NY)])
    give_back(2)
    for i in (0, 1):
        q_all(i).wait_recv()
        unit([(0, 0, i), (0, 1, i)], first=1)
    for d in (1, 3):
        for a in (K, V):
            y_copy(0, a, d).wait_recv()
        unit([(d, half, i) for i in (0, 1) for half in (0, 1)])
    combine(2)
    for a in (K, V):
        y_copy(0, a, 2).wait_recv()
    for i in (0, 1):
        unit([(2, 0, i), (2, 1, i)])
        give_back(i)

    for i in range(SETS):
        for a in range(3):
            entry_all(a, i).wait_send()
        q_all(i).wait_send()
    for a in (K, V):
        y_all(0, a).wait_send()
        y_all(1, a).wait_send()
        c_all(a).wait_send()
    combine(0)
    combine(1)
    for i in range(SETS):
        o_all(i).wait_send()
    for i in (2, 0, 1):
        fin_all(i).wait_recv()
    for s in range(H):
        out_ref[:, s * HD:(s + 1) * HD] = got[plan_s[s]]
    for i in range(SETS):
        fin_all(i).wait_send()


def body(queries, keys, values, block_mask, plan):
    dma = pltpu.SemaphoreType.DMA
    hbm, smem = pl.BlockSpec(memory_space=pl.ANY), pl.BlockSpec(memory_space=pltpu.SMEM)
    return pl.pallas_call(
        kernel,
        out_shape=jax.ShapeDtypeStruct(queries.shape, BF),
        in_specs=[hbm, hbm, hbm, hbm, smem],
        out_specs=pl.BlockSpec(memory_space=pltpu.VMEM),
        scratch_shapes=[
            pltpu.VMEM((2, NY, 2, RUN, HD), BF),
            pltpu.VMEM((2, NY, 2, RUN, HD), BF),
            pltpu.VMEM((SETS, RUN, HD), BF),
            pltpu.VMEM((SETS, LANES, HD), BF),
            pltpu.VMEM((HL, NB, NB), jnp.int32),
            pltpu.VMEM((2, NY, NZ, LANES), F32),
            pltpu.VMEM((SETS, HD, LANES), F32),
            pltpu.VMEM((SETS, 1, LANES), F32),
            pltpu.VMEM((SETS, 1, LANES), F32),
            pltpu.VMEM((SETS, NX - 1, HD + 16, RUN), BF),
            pltpu.VMEM((SETS, NX - 1, HD + 16, RUN), BF),
            pltpu.VMEM((SETS, RUN, HD), BF),
            pltpu.VMEM((H, TD, HD), BF),
            dma((3, SETS)), dma((3, SETS)), dma((3, SETS)), dma,
            dma((2, 2)), dma((2, 2, NY - 1)),
            dma((2,)), dma((2, NY)),
            dma((SETS,)), dma((SETS,)),
            dma((SETS,)), dma((SETS,)),
            dma((SETS,)), dma((SETS,)),
        ],
        compiler_params=pltpu.CompilerParams(
            collective_id=0, has_side_effects=True, vmem_limit_bytes=VMEM_MIB * 1024 * 1024
        ),
    )(queries, keys, values, block_mask, plan)


def solution(mesh):
    placed = (P(("blk", "uly"), None), P(("blk", "uly"), None), P(("blk", "uly"), None), P(), P())
    return jax.shard_map(
        body, mesh=mesh, in_specs=placed, out_specs=P(("blk", "uly"), None), check_vma=False
    )
```

time: 704 us -> 55.8 us (0.08)
  waiting for transfers between devices: 569 us -> 0 us
  Pallas kernels: 0 us -> 54.1 us
  starting transfers between devices: 53 us -> 0 us
  matrix products: 27.8 us -> 0 us
  blocking collectives: 20.9 us -> 0 us
  between operations: 13.5 us -> 0.01 us
  other arithmetic: 12.9 us -> 0 us
    all_gather x2 -> x0, waiting for transfers between devices: 557 us -> none  [the longest x1 297 us: body(): v_piece = lax.all_gather(v_head, 'blk', axis=0, tiled=True)]
    pallas_call x0 -> x1, Pallas kernels: none -> 54.1 us  [body(): pl.pallas_call(kernel, out_shape=jax.ShapeDtypeStruct(queries.shape, BF),...]
    all_to_all x2 -> x0, starting transfers between devices: 52.9 us -> none  [the longest x1 48.9 us: body(): lax.all_to_all(result, 'uly', split_axis=0, concat_axis=1, tiled=True)]
    dot_general x2 -> x0, matrix products: 27.8 us -> none  [the longest x1 14.9 us: body(): jnp.einsum('hqk,khd->hqd', expo.astype(jnp.bfloat16), v_piece, preferred_...]
    all_to_all x2 -> x0, blocking collectives: 20.9 us -> none  [the longest x1 11.7 us: body(): lax.all_to_all(k_tok, 'uly', split_axis=1, concat_axis=0, tiled=True)]
    all_to_all x2 -> x0, waiting for transfers between devices: 11.8 us -> none  [the longest x1 6.66 us: body(): lax.all_to_all(result, 'uly', split_axis=0, concat_axis=1, tiled=True)]
    reduce_sum x1 -> x0, other arithmetic: 11.5 us -> none  [body(): total = jnp.sum(expo, axis=2)]
  transfers between devices with their start and end apart: 4 -> 0, of which waited for: 4 -> 0; matrix products, arithmetic and copies ran while one was open for 4% -> 0% of each run, Pallas kernels for 0% -> 0%
where the time goes in v4:
time: 55.8 us; the launch traced here: 55.7 us
  Pallas kernels  54.1 us (97%)
  local copies, waits for them, and re-layouts  1.62 us (3%)
    pallas_call x1, Pallas kernels, body(): pl.pallas_call(kernel, out_shape=jax.ShapeDtypeStruct(queries.shape, BF),...  54.1 us
    unnamed x1, local copies, waits for them, and re-layouts  1.62 us

profile of v4, /device:TPU:1, one launch (start us, length us, event | category | flops | bytes accessed | tf_op | source)
XLA Modules:
  0.0 55.7 jit_solution(10399670632088601852)
XLA Ops:
  0.0 54.1 %shard_map.55 = bf16[32,3072]{1,0:T(8,128)(2,1)} custom-call(bf16[32,3072]{1,0:T(8,128)(2,1)} %q_in.1, bf16[32,3072]{1,0:T(8,128)(2,1)} %k_in.1, bf16[32,3072]{1,0:T(8,128)(2,1)} %v_in.1, s32[24,64,64]{2,1,0:T(8,128)} %mask_in.1, s32[24]{0:T(128)} %plan_s.1), custom_call_target="tpu_custom_call" | custom-call | tf_op jit(solution)/shard_map/pallas_call | solution.py:328
  54.1 1.6 %copy.7 = bf16[32,3072]{1,0:T(8,128)(2,1)} copy(bf16[32,3072]{1,0:T(8,128)(2,1)} %shard_map.55) | data formatting | bytes 393216

commit v5 on v4

--- a/solution.py
+++ b/solution.py
@@ -25,9 +25,9 @@
 
 
 def kernel(
-    q_in, k_in, v_in, mask_in, plan_s, out_ref,
-    kb, vb, v_st, q_buf, m_st, shade, acc, top, tot, ob, ob_in, fin, got,
-    us, ur, ul, ml, ys, yr, cs, cr, qs, qr, os_, or_, fs, fr,
+    q_in, k_in, v_in, mask_in, got,
+    kb, vb, v_st, q_buf, m_st, shade, acc, top, tot, ob, ob_in, fin,
+    us, ur, ul, ml, ys, yr, cs, cr, qs, qr, os_, or_, fs, fr, fl,
 ):
     u = lax.axis_index("uly")
     b = lax.axis_index("blk")
@@ -102,14 +102,15 @@
             own_in(a, i).wait()
         entry_all(a, i).wait_recv()
 
-    def y_copy(hk, a, d):
+    def y_copy(hk, a, half, d):
         buf = vb if a == V else kb
-        src, dst = (buf.at[0, 0], buf.at[0, d]) if hk == 0 else (buf.at[1, 0, 0], buf.at[1, d, 0])
-        return remote(src, dst, ys.at[hk, a], yr.at[hk, a, d - 1], y_side[NY - d])
+        return remote(
+            buf.at[hk, 0, half], buf.at[hk, d, half], ys.at[hk, a], yr.at[hk, a, half, d - 1], y_side[NY - d]
+        )
 
     def y_all(hk, a):
         ref = kb.at[0, 1:NY] if hk == 0 else kb.at[1, 1:NY, 0]
-        return sum_of(ref, ys.at[hk, a], yr.at[hk, a, 0])
+        return sum_of(ref, ys.at[hk, a], yr.at[hk, a, 0, 0])
 
     def c_copy(a, d):
         buf = vb if a == V else kb
@@ -138,6 +139,9 @@
         rows = pl.ds(pl.multiple_of(((z + k) % NZ) * TD, TD), TD)
         device = cross[k] if i == 1 else same[k]
         return remote(fin.at[i, rows, :], got.at[mine[i]], fs.at[i], fr.at[i], device)
+
+    def own_out(i):
+        return pltpu.make_async_copy(fin.at[i, here, :], got.at[mine[i]], fl.at[i])
 
     def fin_all(i):
         return sum_of(got.at[0:NZ - first_of(i)], fs.at[i], fr.at[i])
@@ -225,25 +229,39 @@
         for k in range(first_of(i), NZ):
             fin_copy(i, k).start()
         if i != 1:
-            got[mine[i]] = fin[i, here, :]
-
-    for a in (K, V, Q):
-        send_in(a, 2)
+            own_out(i).start()
+
     for a in (K, Q, V):
         send_in(a, 0)
         send_in(a, 1)
-
+    for a in (K, V, Q):
+        send_in(a, 2)
+
+    for i in (0, 1):
+        arrive(K, i)
+    for d in (2, 1, 3):
+        y_copy(0, K, 0, d).start()
+        y_copy(0, K, 1, d).start()
+    for i in (0, 1):
+        arrive(Q, i)
+        for d in (2, 1, 3):
+            q_copy(i, d).start()
+    for i in (0, 1):
+        arrive(V, i)
+        turn(i)
+        for d in (2, 1, 3):
+            y_copy(0, V, i, d).start()
     arrive(K, 2)
-    for d in range(1, NY):
-        y_copy(1, K, d).start()
+    for d in (2, 1, 3):
+        y_copy(1, K, 0, d).start()
     c_copy(K, 0).start()
     arrive(V, 2)
     turn(2)
-    for d in range(1, NY):
-        y_copy(1, V, d).start()
+    for d in (2, 1, 3):
+        y_copy(1, V, 0, d).start()
     c_copy(V, 0).start()
     arrive(Q, 2)
-    for d in range(1, NX):
+    for d in (2, 1, 3):
         q_copy(2, d).start()
 
     mask_copy.wait()
@@ -264,44 +282,33 @@
             shade[hk, d] = rows[d * NZ:(d + 1) * NZ, :]
 
     for i in (0, 1):
-        arrive(K, i)
-    for d in range(1, NY):
-        y_copy(0, K, d).start()
-    for i in (0, 1):
-        arrive(Q, i)
-        for d in range(1, NX):
-            q_copy(i, d).start()
-    for i in (0, 1):
-        arrive(V, i)
-        turn(i)
-    for d in range(1, NY):
-        y_copy(0, V, d).start()
-
-    for d in (1, 3, 2):
-        for a in (K, V):
-            y_copy(1, a, d).wait_recv()
-            c_copy(a, d).start()
+        q_all(i).wait_recv()
+    unit([(0, half, i) for half in (0, 1) for i in (0, 1)], first=2)
+    for half in (0, 1):
+        for d in (2, 1, 3):
+            y_copy(0, K, half, d).wait_recv()
+            y_copy(0, V, half, d).wait_recv()
+            unit([(d, half, i) for i in (0, 1)])
+    for i in (0, 1):
+        give_back(i)
+    for d in (2, 1, 3):
+        y_copy(1, K, 0, d).wait_recv()
+        c_copy(K, d).start()
     q_all(2).wait_recv()
-    unit([(d, 0, 2) for d in (0, 1, 3, 2)], first=1)
-    for d in range(NY):
+    for a in (K, V):
+        c_copy(a, 0).wait_recv()
+    unit([(0, 0, 2), (0, 1, 2)], first=1)
+    for d in (2, 1, 3):
+        y_copy(1, V, 0, d).wait_recv()
+        c_copy(V, d).start()
+    unit([(d, 0, 2) for d in (2, 1, 3)])
+    for d in (2, 1, 3):
         for a in (K, V):
             c_copy(a, d).wait_recv()
-    unit([(d, 1, 2) for d in range(NY)])
+    unit([(d, 1, 2) for d in (2, 1, 3)])
     give_back(2)
-    for i in (0, 1):
-        q_all(i).wait_recv()
-        unit([(0, 0, i), (0, 1, i)], first=1)
-    for d in (1, 3):
-        for a in (K, V):
-            y_copy(0, a, d).wait_recv()
-        unit([(d, half, i) for i in (0, 1) for half in (0, 1)])
-    combine(2)
-    for a in (K, V):
-        y_copy(0, a, 2).wait_recv()
-    for i in (0, 1):
-        unit([(2, 0, i), (2, 1, i)])
-        give_back(i)
-
+    combine(0)
+    combine(1)
     for i in range(SETS):
         for a in range(3):
             entry_all(a, i).wait_send()
@@ -310,26 +317,25 @@
         y_all(0, a).wait_send()
         y_all(1, a).wait_send()
         c_all(a).wait_send()
-    combine(0)
-    combine(1)
+    combine(2)
     for i in range(SETS):
         o_all(i).wait_send()
-    for i in (2, 0, 1):
+    for i in range(SETS):
         fin_all(i).wait_recv()
-    for s in range(H):
-        out_ref[:, s * HD:(s + 1) * HD] = got[plan_s[s]]
     for i in range(SETS):
         fin_all(i).wait_send()
+        if i != 1:
+            own_out(i).wait()
 
 
 def body(queries, keys, values, block_mask, plan):
     dma = pltpu.SemaphoreType.DMA
-    hbm, smem = pl.BlockSpec(memory_space=pl.ANY), pl.BlockSpec(memory_space=pltpu.SMEM)
-    return pl.pallas_call(
+    hbm = pl.BlockSpec(memory_space=pl.ANY)
+    heads = pl.pallas_call(
         kernel,
-        out_shape=jax.ShapeDtypeStruct(queries.shape, BF),
-        in_specs=[hbm, hbm, hbm, hbm, smem],
-        out_specs=pl.BlockSpec(memory_space=pltpu.VMEM),
+        out_shape=jax.ShapeDtypeStruct((H, TD, HD), BF),
+        in_specs=[hbm, hbm, hbm, hbm],
+        out_specs=hbm,
         scratch_shapes=[
             pltpu.VMEM((2, NY, 2, RUN, HD), BF),
             pltpu.VMEM((2, NY, 2, RUN, HD), BF),
@@ -343,18 +349,18 @@
             pltpu.VMEM((SETS, NX - 1, HD + 16, RUN), BF),
             pltpu.VMEM((SETS, NX - 1, HD + 16, RUN), BF),
             pltpu.VMEM((SETS, RUN, HD), BF),
-            pltpu.VMEM((H, TD, HD), BF),
             dma((3, SETS)), dma((3, SETS)), dma((3, SETS)), dma,
-            dma((2, 2)), dma((2, 2, NY - 1)),
+            dma((2, 2)), dma((2, 2, 2, NY - 1)),
             dma((2,)), dma((2, NY)),
             dma((SETS,)), dma((SETS,)),
             dma((SETS,)), dma((SETS,)),
-            dma((SETS,)), dma((SETS,)),
+            dma((SETS,)), dma((SETS,)), dma((SETS,)),
         ],
         compiler_params=pltpu.CompilerParams(
             collective_id=0, has_side_effects=True, vmem_limit_bytes=VMEM_MIB * 1024 * 1024
         ),
-    )(queries, keys, values, block_mask, plan)
+    )(queries, keys, values, block_mask)
+    return jnp.transpose(heads.at[plan].get(mode="promise_in_bounds"), (1, 0, 2)).reshape(queries.shape)
 
 
 def solution(mesh):

time: 55.8 us -> 53.3 us (0.955)
  Pallas kernels: 54.1 us -> 50.2 us
  other arithmetic: 0 us -> 0.67 us
  local copies, waits for them, and re-layouts: 1.62 us -> 2.2 us
    pallas_call x1, Pallas kernels: 54.1 us -> 50.2 us  [body(): pl.pallas_call(kernel, out_shape=jax.ShapeDtypeStruct((H, TD, HD), BF), i...]
    unnamed x1 -> x0, local copies, waits for them, and re-layouts: 1.62 us -> none
    gather x0 -> x1, local copies, waits for them, and re-layouts: none -> 1.51 us  [body(): heads.at[plan].get(mode='promise_in_bounds')]
    reshape x0 -> x1, local copies, waits for them, and re-layouts: none -> 0.69 us  [body(): jnp.transpose(heads.at[plan].get(mode='promise_in_bounds'), (1, 0, 2))]
    select_n x0 -> x1, other arithmetic: none -> 0.66 us  [body(): heads.at[plan].get(mode='promise_in_bounds')]
where the time goes in v5:
time: 53.3 us; the launch traced here: 53.1 us
  Pallas kernels  50.2 us (94%)
  local copies, waits for them, and re-layouts  2.2 us (4%)
  other arithmetic  0.67 us (1%)
    pallas_call x1, Pallas kernels, body(): pl.pallas_call(kernel, out_shape=jax.ShapeDtypeStruct((H, TD, HD), BF), i...  50.2 us
    gather x1, local copies, waits for them, and re-layouts, body(): heads.at[plan].get(mode='promise_in_bounds')  1.51 us

profile of v5, /device:TPU:1, one launch (start us, length us, event | category | flops | bytes accessed | tf_op | source)
XLA Modules:
  0.0 53.1 jit_solution(548090103665448834)
XLA Ops:
  0.0 0.7 %compare_select_fusion = s32[24]{0:T(128)S(1)} fusion(s32[24]{0:T(128)} %param.9), kind=kLoop, calls=%fused_computation.3 | loop fusion | flops 72 | bytes 192 | tf_op jit(solution)/shard_map/select_n | solution.py:363
  0.7 50.2 %shard_map.55 = bf16[24,32,128]{2,1,0:T(8,128)(2,1)} custom-call(bf16[32,3072]{1,0:T(8,128)(2,1)} %q_in.1, bf16[32,3072]{1,0:T(8,128)(2,1)} %k_in.1, bf16[32,3072]{1,0:T(8,128)(2,1)} %v_in.1, s32[24,64,64]{2,1,0:T(8,128)} %mask_in.1), custom_call_target="tpu_custom_call" | custom-call | tf_op jit(solution)/shard_map/pallas_call | solution.py:334
  50.9 1.5 %gather_fusion = bf16[24,32,128]{2,1,0:T(8,128)(2,1)S(1)} fusion(bf16[24,32,128]{2,1,0:T(8,128)(2,1)} %shard_map.55, s32[1024]{0:T(1024)S(1)} %pad_clamp_fusion), kind=kCustom, calls=%fused_computation | custom fusion | bytes 393312 | tf_op jit(solution)/shard_map/gather | solution.py:363
  52.4 0.7 %copy_bitcast_fusion = bf16[32,3072]{1,0:T(8,128)(2,1)} fusion(bf16[24,32,128]{2,1,0:T(8,128)(2,1)S(1)} %gather_fusion), kind=kLoop, calls=%fused_computation.1 | loop fusion | bytes 393216 | tf_op jit(solution)/shard_map/reshape | solution.py:363
  (1 shorter events, 0.0 us)

commit v6 on v5

--- a/solution.py
+++ b/solution.py
@@ -204,7 +204,7 @@
 
     def give_back(i):
         row = lax.broadcasted_iota(jnp.int32, (16, RUN), 0)
-        for d in range(1, NX):
+        for d in (2, 1, 3):
             lanes = slice(d * RUN, (d + 1) * RUN)
             ob[i, d - 1, 0:HD, :] = acc[i, :, lanes].astype(BF)
             notes = jnp.zeros((16, RUN), F32)
@@ -239,9 +239,8 @@
 
     for i in (0, 1):
         arrive(K, i)
-    for d in (2, 1, 3):
-        y_copy(0, K, 0, d).start()
-        y_copy(0, K, 1, d).start()
+        for d in (2, 1, 3):
+            y_copy(0, K, i, d).start()
     for i in (0, 1):
         arrive(Q, i)
         for d in (2, 1, 3):
@@ -326,6 +325,11 @@
         fin_all(i).wait_send()
         if i != 1:
             own_out(i).wait()
+
+
+def arrange(plan_s, heads, out):
+    for s in range(H):
+        out[:, s * HD:(s + 1) * HD] = heads[plan_s[s]]
 
 
 def body(queries, keys, values, block_mask, plan):
@@ -360,7 +364,13 @@
             collective_id=0, has_side_effects=True, vmem_limit_bytes=VMEM_MIB * 1024 * 1024
         ),
     )(queries, keys, values, block_mask)
-    return jnp.transpose(heads.at[plan].get(mode="promise_in_bounds"), (1, 0, 2)).reshape(queries.shape)
+    whole = pl.BlockSpec(memory_space=pltpu.VMEM)
+    return pl.pallas_call(
+        arrange,
+        out_shape=jax.ShapeDtypeStruct(queries.shape, BF),
+        in_specs=[pl.BlockSpec(memory_space=pltpu.SMEM), whole],
+        out_specs=whole,
+    )(plan, heads)
 
 
 def solution(mesh):

time: 53.3 us -> 51.7 us (0.970)
  the two profiles are of different devices: /device:TPU:1 before, /device:TPU:8 now
where the time goes in v6:
time: 51.7 us; the launch traced here: 51.6 us
  Pallas kernels  51.6 us (100%)
    pallas_call x1, Pallas kernels, body(): pl.pallas_call(kernel, out_shape=jax.ShapeDtypeStruct((H, TD, HD), BF), i...  49.9 us
    pallas_call x1, Pallas kernels, body(): pl.pallas_call(arrange, out_shape=jax.ShapeDtypeStruct(queries.shape, BF)...  1.66 us

profile of v6, /device:TPU:8, one launch (start us, length us, event | category | flops | bytes accessed | tf_op | source)
XLA Modules:
  0.0 51.6 jit_solution(7519029429436881996)
XLA Ops:
  0.0 49.9 %shard_map.55.heads = bf16[24,32,128]{2,1,0:T(8,128)(2,1)} custom-call(bf16[32,3072]{1,0:T(8,128)(2,1)} %q_in.1, bf16[32,3072]{1,0:T(8,128)(2,1)} %k_in.1, bf16[32,3072]{1,0:T(8,128)(2,1)} %v_in.1, s32[24,64,64]{2,1,0:T(8,128)} %mask_in.1), custom_call_target="tpu_custom_call" | custom-call | tf_op jit(solution)/shard_map/pallas_call | solution.py:338
  49.9 1.7 %shard_map.56 = bf16[32,3072]{1,0:T(8,128)(2,1)} custom-call(s32[24]{0:T(128)} %plan_s.1, bf16[24,32,128]{2,1,0:T(8,128)(2,1)} %shard_map.55.heads), custom_call_target="tpu_custom_call" | custom-call | tf_op jit(solution)/shard_map/pallas_call | solution.py:368

commit v7 on v6

--- a/solution.py
+++ b/solution.py
@@ -83,6 +83,8 @@
     def sum_of(ref, send, recv):
         return remote(ref, ref, send, recv, same[1])
 
+    far = (4, 3, 5, 2, 6, 1, 7)
+
     def first_of(i):
         return 0 if i == 1 else 1
 
@@ -94,7 +96,7 @@
         return sum_of(v_st.at[i, 0:(NZ - first_of(i)) * TD, :], us.at[a, i], ur.at[a, i])
 
     def send_in(a, i):
-        for k in range(first_of(i), NZ):
+        for k in far if i != 1 else far + (0,):
             entry(a, i, k).start()
 
     def arrive(a, i):
@@ -226,7 +228,7 @@
         for d in range(NX - 1):
             mixed = mixed + ob_in[i, d, 0:HD, :].astype(F32) * (fades[d + 1] * share)
         fin[i] = mixed.astype(BF).T
-        for k in range(first_of(i), NZ):
+        for k in far if i != 1 else far + (0,):
             fin_copy(i, k).start()
         if i != 1:
             own_out(i).start()
@@ -283,12 +285,15 @@
     for i in (0, 1):
         q_all(i).wait_recv()
     unit([(0, half, i) for half in (0, 1) for i in (0, 1)], first=2)
-    for half in (0, 1):
-        for d in (2, 1, 3):
-            y_copy(0, K, half, d).wait_recv()
-            y_copy(0, V, half, d).wait_recv()
-            unit([(d, half, i) for i in (0, 1)])
-    for i in (0, 1):
+    for half, d in ((0, 2), (0, 1), (0, 3), (1, 2)):
+        y_copy(0, K, half, d).wait_recv()
+        y_copy(0, V, half, d).wait_recv()
+        unit([(d, half, i) for i in (0, 1)])
+    for d in (1, 3):
+        y_copy(0, K, 1, d).wait_recv()
+        y_copy(0, V, 1, d).wait_recv()
+    for i in (0, 1):
+        unit([(d, 1, i) for d in (1, 3)])
         give_back(i)
     for d in (2, 1, 3):
         y_copy(1, K, 0, d).wait_recv()

time: 51.7 us -> 49.7 us (0.961)
  the two profiles are of different devices: /device:TPU:8 before, /device:TPU:1 now
where the time goes in v7:
time: 49.7 us; the launch traced here: 48.9 us
  Pallas kernels  48.9 us (98%)
    pallas_call x1, Pallas kernels, body(): pl.pallas_call(kernel, out_shape=jax.ShapeDtypeStruct((H, TD, HD), BF), i...  47.3 us
    pallas_call x1, Pallas kernels, body(): pl.pallas_call(arrange, out_shape=jax.ShapeDtypeStruct(queries.shape, BF)...  1.66 us

profile of v7, /device:TPU:1, one launch (start us, length us, event | category | flops | bytes accessed | tf_op | source)
XLA Modules:
  0.0 48.9 jit_solution(11754834332483566711)
XLA Ops:
  0.0 47.3 %shard_map.55.heads = bf16[24,32,128]{2,1,0:T(8,128)(2,1)} custom-call(bf16[32,3072]{1,0:T(8,128)(2,1)} %q_in.1, bf16[32,3072]{1,0:T(8,128)(2,1)} %k_in.1, bf16[32,3072]{1,0:T(8,128)(2,1)} %v_in.1, s32[24,64,64]{2,1,0:T(8,128)} %mask_in.1), custom_call_target="tpu_custom_call" | custom-call | tf_op jit(solution)/shard_map/pallas_call | solution.py:343
  47.3 1.7 %shard_map.56 = bf16[32,3072]{1,0:T(8,128)(2,1)} custom-call(s32[24]{0:T(128)} %plan_s.1, bf16[24,32,128]{2,1,0:T(8,128)(2,1)} %shard_map.55.heads), custom_call_target="tpu_custom_call" | custom-call | tf_op jit(solution)/shard_map/pallas_call | solution.py:373

commit v8 on v7

--- a/solution.py
+++ b/solution.py
@@ -284,7 +284,7 @@
 
     for i in (0, 1):
         q_all(i).wait_recv()
-    unit([(0, half, i) for half in (0, 1) for i in (0, 1)], first=2)
+        unit([(0, half, i) for half in (0, 1)], first=1)
     for half, d in ((0, 2), (0, 1), (0, 3), (1, 2)):
         y_copy(0, K, half, d).wait_recv()
         y_copy(0, V, half, d).wait_recv()

time: 49.7 us -> 50 us (level)
  no operation moved by 1% of the time
where the time goes in v8:
time: 50 us; the launch traced here: 49.3 us
  Pallas kernels  49.3 us (99%)
    pallas_call x1, Pallas kernels, body(): pl.pallas_call(kernel, out_shape=jax.ShapeDtypeStruct((H, TD, HD), BF), i...  47.7 us
    pallas_call x1, Pallas kernels, body(): pl.pallas_call(arrange, out_shape=jax.ShapeDtypeStruct(queries.shape, BF)...  1.66 us

profile of v8, /device:TPU:1, one launch (start us, length us, event | category | flops | bytes accessed | tf_op | source)
XLA Modules:
  0.0 49.3 jit_solution(5556649702964463846)
XLA Ops:
  0.0 47.7 %shard_map.55.heads = bf16[24,32,128]{2,1,0:T(8,128)(2,1)} custom-call(bf16[32,3072]{1,0:T(8,128)(2,1)} %q_in.1, bf16[32,3072]{1,0:T(8,128)(2,1)} %k_in.1, bf16[32,3072]{1,0:T(8,128)(2,1)} %v_in.1, s32[24,64,64]{2,1,0:T(8,128)} %mask_in.1), custom_call_target="tpu_custom_call" | custom-call | tf_op jit(solution)/shard_map/pallas_call | solution.py:343
  47.7 1.7 %shard_map.56 = bf16[32,3072]{1,0:T(8,128)(2,1)} custom-call(s32[24]{0:T(128)} %plan_s.1, bf16[24,32,128]{2,1,0:T(8,128)(2,1)} %shard_map.55.heads), custom_call_target="tpu_custom_call" | custom-call | tf_op jit(solution)/shard_map/pallas_call | solution.py:373
